TPU v7x, 512 devices: a whole 4x8x8 slice. The times are simulated.
512 devices in a mesh: row: 32 (over y, x), col: 16 (over z, core).
Axes of the slice: x: 4, y: 8, z: 8, core: 2. Of those that a mesh axis runs over, the one named last changes fastest.
Arguments:
- gradient: float32 [6144, 24576], P('row', 'col'), as said below
Outputs:
- update: float32 [6144, 24576], P('row', 'col')
Inputs may be any that keep to these rules, and one draw needn't show every extreme that they name: `gradient`: each entry is a random value times a row scale times a column scale.
All inputs are finite; a program needn't handle non-finite values.
Results may differ from a plain program's by a relative error of at most 0.0003.
Values sent between devices are 32-bit elements; how exact they have to be, the bound alone decides.
No kernel may reach another device: no remote copies, remote signals or barrier semaphores. Data moves between devices by JAX's collectives and lax.ppermute only.
A program may use at most 64 MiB of HBM per device.

v0:
```python
import jax
import jax.numpy as jnp
from jax import lax
from jax.sharding import PartitionSpec as P

D_IN = 6144
D_OUT = 24576
BLOCK = 192
ITERS = 12


def spread(x, axis, root):
    mine = lax.axis_index(axis) == root
    return lax.psum(jnp.where(mine, x, jnp.zeros_like(x)), axis)


def batch_product(left, right):
    return jnp.einsum("bij,bjk->bik", left, right, precision=lax.Precision.HIGHEST)


def root_blocks(gram):
    order = gram.shape[-1]
    identity = jnp.eye(order, dtype=jnp.float32)
    diag_total = jnp.trace(gram, axis1=1, axis2=2)
    damped = gram + (0.01 * diag_total / order)[:, None, None] * identity
    scale_by_norm = jnp.sqrt(jnp.sum(damped * damped, axis=(1, 2)))
    current = damped / scale_by_norm[:, None, None]
    root_est = identity * (scale_by_norm ** (-0.25))[:, None, None]

    def newton_step(iteration, state):
        root_est, current = state
        factor = (5.0 * identity - current) * 0.25
        root_est = batch_product(root_est, factor)
        square = batch_product(factor, factor)
        current = batch_product(batch_product(square, square), current)
        return (root_est, current)

    root_est, current = lax.fori_loop(0, ITERS, newton_step, (root_est, current))
    return root_est


def skip_blocks(held):
    return jnp.zeros_like(held)


def owned_roots(gram, position, axis_count):
    block_count = gram.shape[0]
    slot_count = max(block_count // axis_count, 1)
    owner_count = min(axis_count, block_count)
    first_block = position * slot_count
    begin = jnp.minimum(first_block, block_count - slot_count)
    owned_gram = lax.dynamic_slice_in_dim(gram, begin, slot_count, 0)
    computed = lax.cond(first_block < block_count, root_blocks, skip_blocks, owned_gram)
    return (computed, slot_count, owner_count)


def body(gradient):
    row_width = gradient.shape[0]
    col_width = gradient.shape[1]
    left_count = row_width // BLOCK
    right_count = col_width // BLOCK
    row_blocks = gradient.reshape(left_count, BLOCK, col_width)
    column_blocks = gradient.reshape(row_width, right_count, BLOCK)
    left_part = jnp.einsum("bid,bjd->bij", row_blocks, row_blocks, precision=lax.Precision.HIGHEST)
    right_block_piece = jnp.einsum(
        "gzy,gzo->zyo", column_blocks, column_blocks, precision=lax.Precision.HIGHEST
    )
    left_gram = lax.psum(left_part, "col")
    right_gram_matrix = lax.psum(right_block_piece, "row")
    left_mine, left_slots, left_owners = owned_roots(
        left_gram, lax.axis_index("col"), lax.axis_size("col")
    )

    def left_owner(owner_rank, buffer):
        received = spread(left_mine, "col", owner_rank)
        return lax.dynamic_update_slice_in_dim(buffer, received, owner_rank * left_slots, 0)

    left_roots = lax.fori_loop(0, left_owners, left_owner, jnp.zeros_like(left_gram))
    right_mine, right_slots, right_owners = owned_roots(
        right_gram_matrix, lax.axis_index("row"), lax.axis_size("row")
    )

    def right_owner(owner_rank, buffer):
        received = spread(right_mine, "row", owner_rank)
        return lax.dynamic_update_slice_in_dim(buffer, received, owner_rank * right_slots, 0)

    right_inverse_roots = lax.fori_loop(
        0, right_owners, right_owner, jnp.zeros_like(right_gram_matrix)
    )
    midpoint_estimate = jnp.einsum(
        "bij,bjd->bid", left_roots, row_blocks, precision=lax.Precision.HIGHEST
    )
    midpoint_estimate = midpoint_estimate.reshape(row_width, right_count, BLOCK)
    update = jnp.einsum(
        "gul,ulb->gub", midpoint_estimate, right_inverse_roots, precision=lax.Precision.HIGHEST
    )
    return update.reshape(row_width, col_width) * (float(D_IN) * float(D_OUT)) ** 0.25


def solution(mesh):
    return jax.shard_map(
        body,
        mesh=mesh,
        in_specs=(P("row", "col"),),
        out_specs=P("row", "col"),
        check_vma=False,
    )
```

profile of v0, /device:TPU:16, one launch (start us, length us, event | category | flops | bytes accessed | tf_op | source)
XLA Modules:
  0.0 1739.6 jit_solution(16200118062168557227)
XLA Ops:
  6.5 3.5 convolution_bitcast_fusion.4
  10.6 114.3 %all-reduce.7.cloned.1.call-done = f32[1,192,192]{2,1,0:T(8,128)} async-done(((f32[1,192,192]{2,1,0:T(8,128)}), f32[1,192,192]{2,1,0:T(8,128)}) %all-reduce.7.cloned.1.call-update) | async-done | bytes 147472 | tf_op jit(solution)/shard_map/psum | solution.py:68
  124.9 45.0 %conditional.3 = (f32[1,192,192]{1,2,0:T(8,128)}) conditional(s32[]{:T(128)} %convert_element_type.19, () %tuple.51, f32[1,192,192]{2,1,0:T(8,128)} %all-reduce.7.cloned.1.call-done), branch_computations={%region_11.12_spmd, %region_12.17_spmd} | conditional | flops 340549632 | bytes 3096733 | solution.py:53
  131.2 38.7 %while.49 = (s32[]{:T(128)}, f32[1,192,192]{1,2,0:T(8,128)}, f32[1,192,192]{2,1,0:T(8,128)S(1)}, s32[]{:T(128)}) while((s32[]{:T(128)}, f32[1,192,192]{1,2,0:T(8,128)}, f32[1,192,192]{2,1,0:T(8,128)S(1)}, s32[]{:T(128)}) %tuple.87), condition=%wide.region_16.16_spmd.clone, body=%wide.region_15.15_spmd.clone.sunk | while | flops 340033536 | bytes 2064437 | solution.py:38
  169.9 1.6 select_bitcast_fusion
  171.6 4.9 fusion.50
  177.0 100.7 %all-reduce.9.cloned.1.call-done = f32[192,192]{0,1:T(8,128)} async-done(((f32[192,192]{0,1:T(8,128)}), f32[192,192]{0,1:T(8,128)}) %all-reduce.9.cloned.1.call-update) | async-done | bytes 147472 | tf_op jit(solution)/shard_map/while/body/eval_jaxpr/psum | solution.py:14
  277.7 2.8 fusion.48
  280.5 162.4 %all-reduce.5.cloned.1.call-done = f32[8,192,192]{2,1,0:T(8,128)} async-done(((f32[8,192,192]{2,1,0:T(8,128)}), f32[8,192,192]{2,1,0:T(8,128)}) %all-reduce.5.cloned.1.call-update) | async-done | bytes 1179664 | tf_op jit(solution)/shard_map/psum | solution.py:69
  443.1 1284.0 %while.50 = (s32[]{:T(128)}, f32[8,192,192]{2,1,0:T(8,128)}, f32[1,192,192]{2,1,0:T(8,128)S(1)}, s32[]{:T(128)}, u32[]{:T(128)}, /*index=5*/u32[]{:T(128)}) while((s32[]{:T(128)}, f32[8,192,192]{2,1,0:T(8,128)}, f32[1,192,192]{2,1,0:T(8,128)S(1)}, s32[]{:T(128)}, u32[]{:T(128)}, /*index=5*/u32[]{:T(128)}) %tuple.95), condition=%wide.region_9.10_spmd, body=%wide.region_7.0_spmd.sunk | while | flops 73734 | bytes 1671331 | solution.py:87
  443.9 178.0 %all-reduce.11.cloned.1.call-done = f32[1,192,192]{2,1,0:T(8,128)} async-done(((f32[1,192,192]{2,1,0:T(8,128)}), f32[1,192,192]{2,1,0:T(8,128)}) %all-reduce.11.cloned.1.call-update) | async-done | bytes 147472 | tf_op jit(solution)/shard_map/while/body/eval_jaxpr/psum | solution.py:14
  624.2 155.1 %all-reduce.11.cloned.1.call-done = f32[1,192,192]{2,1,0:T(8,128)} async-done(((f32[1,192,192]{2,1,0:T(8,128)}), f32[1,192,192]{2,1,0:T(8,128)}) %all-reduce.11.cloned.1.call-update) | async-done | bytes 147472 | tf_op jit(solution)/shard_map/while/body/eval_jaxpr/psum | solution.py:14
  779.4 1.6 constant_dynamic-update-slice_fusion.2
  781.7 155.1 %all-reduce.11.cloned.1.call-done = f32[1,192,192]{2,1,0:T(8,128)} async-done(((f32[1,192,192]{2,1,0:T(8,128)}), f32[1,192,192]{2,1,0:T(8,128)}) %all-reduce.11.cloned.1.call-update) | async-done | bytes 147472 | tf_op jit(solution)/shard_map/while/body/eval_jaxpr/psum | solution.py:14
  939.2 155.4 %all-reduce.11.cloned.1.call-done = f32[1,192,192]{2,1,0:T(8,128)} async-done(((f32[1,192,192]{2,1,0:T(8,128)}), f32[1,192,192]{2,1,0:T(8,128)}) %all-reduce.11.cloned.1.call-update) | async-done | bytes 147472 | tf_op jit(solution)/shard_map/while/body/eval_jaxpr/psum | solution.py:14
  1094.6 1.6 constant_dynamic-update-slice_fusion.2
  1097.0 155.4 %all-reduce.11.cloned.1.call-done = f32[1,192,192]{2,1,0:T(8,128)} async-done(((f32[1,192,192]{2,1,0:T(8,128)}), f32[1,192,192]{2,1,0:T(8,128)}) %all-reduce.11.cloned.1.call-update) | async-done | bytes 147472 | tf_op jit(solution)/shard_map/while/body/eval_jaxpr/psum | solution.py:14
  1252.4 1.6 constant_dynamic-update-slice_fusion.2
  1254.8 155.4 %all-reduce.11.cloned.1.call-done = f32[1,192,192]{2,1,0:T(8,128)} async-done(((f32[1,192,192]{2,1,0:T(8,128)}), f32[1,192,192]{2,1,0:T(8,128)}) %all-reduce.11.cloned.1.call-update) | async-done | bytes 147472 | tf_op jit(solution)/shard_map/while/body/eval_jaxpr/psum | solution.py:14
  1412.5 155.1 %all-reduce.11.cloned.1.call-done = f32[1,192,192]{2,1,0:T(8,128)} async-done(((f32[1,192,192]{2,1,0:T(8,128)}), f32[1,192,192]{2,1,0:T(8,128)}) %all-reduce.11.cloned.1.call-update) | async-done | bytes 147472 | tf_op jit(solution)/shard_map/while/body/eval_jaxpr/psum | solution.py:14
  1567.7 1.6 constant_dynamic-update-slice_fusion.2
  1570.0 155.4 %all-reduce.11.cloned.1.call-done = f32[1,192,192]{2,1,0:T(8,128)} async-done(((f32[1,192,192]{2,1,0:T(8,128)}), f32[1,192,192]{2,1,0:T(8,128)}) %all-reduce.11.cloned.1.call-update) | async-done | bytes 147472 | tf_op jit(solution)/shard_map/while/body/eval_jaxpr/psum | solution.py:14
  1725.5 1.6 constant_dynamic-update-slice_fusion.2
  1727.1 4.5 convolution_multiply_fusion
  (118 shorter events, 56.4 us)
Async XLA Ops:
  6.5 3.6 copy-start
  6.5 118.4 %all-reduce.7.cloned.1.call-start = ((), (), s32[]{:S(2)}) async-start(), calls=%async_computation.1 | async-start | bytes 393216 | tf_op jit(solution)/shard_map/psum | solution.py:68
  10.1 267.6 %all-reduce.9.cloned.1.call-start = ((), (), s32[]{:S(2)}) async-start(), calls=%async_computation.2 | async-start | bytes 393216 | tf_op jit(solution)/shard_map/while/body/eval_jaxpr/psum | solution.py:14
  171.6 271.3 %all-reduce.5.cloned.1.call-start = ((), (), s32[]{:S(2)}) async-start(), calls=%async_computation | async-start | bytes 3145728 | tf_op jit(solution)/shard_map/psum | solution.py:69
  443.1 178.8 %all-reduce.11.cloned.1.call-start = ((), (), s32[]{:S(2)}) async-start(), calls=%async_computation.3 | async-start | bytes 393216 | tf_op jit(solution)/shard_map/while/body/eval_jaxpr/psum | solution.py:14
  623.5 155.9 %all-reduce.11.cloned.1.call-start = ((), (), s32[]{:S(2)}) async-start(), calls=%async_computation.3 | async-start | bytes 393216 | tf_op jit(solution)/shard_map/while/body/eval_jaxpr/psum | solution.py:14
  781.0 155.9 %all-reduce.11.cloned.1.call-start = ((), (), s32[]{:S(2)}) async-start(), calls=%async_computation.3 | async-start | bytes 393216 | tf_op jit(solution)/shard_map/while/body/eval_jaxpr/psum | solution.py:14
  938.5 156.2 %all-reduce.11.cloned.1.call-start = ((), (), s32[]{:S(2)}) async-start(), calls=%async_computation.3 | async-start | bytes 393216 | tf_op jit(solution)/shard_map/while/body/eval_jaxpr/psum | solution.py:14
  1096.3 156.2 %all-reduce.11.cloned.1.call-start = ((), (), s32[]{:S(2)}) async-start(), calls=%async_computation.3 | async-start | bytes 393216 | tf_op jit(solution)/shard_map/while/body/eval_jaxpr/psum | solution.py:14
  1254.0 156.2 %all-reduce.11.cloned.1.call-start = ((), (), s32[]{:S(2)}) async-start(), calls=%async_computation.3 | async-start | bytes 393216 | tf_op jit(solution)/shard_map/while/body/eval_jaxpr/psum | solution.py:14
  1411.8 155.9 %all-reduce.11.cloned.1.call-start = ((), (), s32[]{:S(2)}) async-start(), calls=%async_computation.3 | async-start | bytes 393216 | tf_op jit(solution)/shard_map/while/body/eval_jaxpr/psum | solution.py:14
  1569.3 156.2 %all-reduce.11.cloned.1.call-start = ((), (), s32[]{:S(2)}) async-start(), calls=%async_computation.3 | async-start | bytes 393216 | tf_op jit(solution)/shard_map/while/body/eval_jaxpr/psum | solution.py:14
Sparse Core Ops, SparseCore 0:
  10.2 114.6 all-reduce.6
  171.7 105.9 all-reduce.8
  281.1 161.7 all-reduce.4
  447.4 174.4 all-reduce.10
  627.8 151.5 all-reduce.10
  785.3 151.5 all-reduce.10
  943.1 151.5 all-reduce.10
  1100.9 151.5 all-reduce.10
  1258.7 151.5 all-reduce.10
  1416.1 151.5 all-reduce.10
  1573.9 151.5 all-reduce.10
where the time goes:
time: 1740 us
  waiting for transfers between devices  1640 us (94%)
  matrix products  42.5 us (2%)
  local copies, waits for them, and re-layouts  27.5 us (2%)
    psum x9, waiting for transfers between devices, spread(): return lax.psum(jnp.where(mine, x, jnp.zeros_like(x)), axis)  1370 us
    psum x1, waiting for transfers between devices, body(): right_gram_matrix = lax.psum(right_block_piece, 'row')  162 us
    psum x1, waiting for transfers between devices, body(): left_gram = lax.psum(left_part, 'col')  114 us
  transfers between devices with their start and end apart: 11, of which 11 were waited for; matrix products, arithmetic and copies ran while one was open for 0% of the time, Pallas kernels for 0%

commit v1 on v0

v1 whole, which is shorter than its diff:
```python
import functools

import jax
import jax.numpy as jnp
from jax import lax
from jax.experimental import pallas as pl
from jax.experimental.pallas import tpu as pltpu
from jax.sharding import Mesh, PartitionSpec as P

D_IN = 6144
D_OUT = 24576
BLOCK = 192
ITERS = 12
HALF = 64
LANES = 128
SCALE = (float(D_IN) * float(D_OUT)) ** 0.25
VMEM = pltpu.CompilerParams(vmem_limit_bytes=40 * 2**20)


def split(a):
    high = a.astype(jnp.bfloat16)
    return high, (a - high.astype(jnp.float32)).astype(jnp.bfloat16)


def product(left, right, dims=((1,), (0,))):
    dot = lambda a, b: lax.dot_general(a, b, (dims, ((), ())), preferred_element_type=jnp.float32)
    return dot(left[0], right[0]) + (dot(left[0], right[1]) + dot(left[1], right[0]))


def pack(a):
    return jnp.concatenate(
        [
            a[:64, :128],
            jnp.concatenate([a[:64, 128:], a[64:128, 64:128]], axis=1),
            jnp.concatenate([a[64:128, 128:], a[128:, 128:]], axis=1),
        ],
        axis=0,
    )


def unpack(p):
    a11, a12 = p[:64, :64], p[:64, 64:]
    a13, a22 = p[64:128, :64], p[64:128, 64:]
    a23, a33 = p[128:, :64], p[128:, 64:]
    return jnp.concatenate(
        [
            jnp.concatenate([a11, a12, a13], axis=1),
            jnp.concatenate([a12.T, a22, a23], axis=1),
            jnp.concatenate([a13.T, a23.T, a33], axis=1),
        ],
        axis=0,
    )


def left_gram_kernel(grad_ref, out_ref):
    g = split(grad_ref[...])
    out_ref[...] = pack(product(g, g, ((1,), (1,))))


def right_gram_kernel(grad_ref, out_ref):
    for c in range(out_ref.shape[0]):
        h = split(grad_ref[:, c * BLOCK : (c + 1) * BLOCK])
        out_ref[c] = pack(product(h, h, ((0,), (0,))))


def newton(gram, m_ref, x_ref):
    rows = lax.broadcasted_iota(jnp.int32, (BLOCK, BLOCK), 0)
    columns = lax.broadcasted_iota(jnp.int32, (BLOCK, BLOCK), 1)
    identity = (rows == columns).astype(jnp.float32)
    damped = gram + (0.01 / BLOCK * jnp.sum(gram * identity)) * identity
    norm = jnp.sqrt(jnp.sum(damped * damped, keepdims=True))
    m = damped / norm

    def advance(m):
        f = split((5.0 * identity - m) * 0.25)
        square = split(product(f, f))
        fourth = split(product(square, square))
        return f, product(fourth, split(m))

    x_ref[...] = (5.0 * identity - m) * 0.25
    m_ref[...] = advance(m)[1]

    def step(k, carry):
        f, m = advance(m_ref[...])
        m_ref[...] = m
        x_ref[...] = product(split(x_ref[...]), f)
        return carry

    lax.fori_loop(0, ITERS - 2, step, 0)
    f = split((5.0 * identity - m_ref[...]) * 0.25)
    return product(split(x_ref[...]), f) * lax.rsqrt(jnp.sqrt(norm))


def right_root_kernel(parts_ref, root_ref, m_ref, x_ref):
    total = parts_ref[0]
    for k in range(1, parts_ref.shape[0]):
        total = total + parts_ref[k]
    root_ref[...] = pack(newton(unpack(total), m_ref, x_ref))


def left_root_kernel(gram_ref, grad_ref, mid_ref, m_ref, x_ref):
    root = split(newton(unpack(gram_ref[...]), m_ref, x_ref))
    for c in range(0, grad_ref.shape[1], 512):
        mid_ref[:, c : c + 512] = product(root, split(grad_ref[:, c : c + 512]))


def update_kernel(mid_ref, roots_ref, out_ref):
    for c in range(roots_ref.shape[0]):
        window = slice(c * BLOCK, (c + 1) * BLOCK)
        root = split(unpack(roots_ref[c]))
        out_ref[:, window] = product(split(mid_ref[:, window]), root) * SCALE


def f32(*shape):
    return jax.ShapeDtypeStruct(shape, jnp.float32)


def estimate(flops):
    return pl.CostEstimate(flops=flops, bytes_accessed=2**20, transcendentals=0)


def shift(x, axis, by):
    n = lax.axis_size(axis)
    return lax.ppermute(x, axis, [(i, (i + by) % n) for i in range(n)])


def copies(x, axes, n):
    return lax.all_to_all(jnp.broadcast_to(x[None], (n,) + x.shape), axes, 0, 0, tiled=True)


def body(gradient):
    height, width = gradient.shape
    count = width // BLOCK
    scratch = [pltpu.VMEM((BLOCK, BLOCK), jnp.float32)] * 2
    group = ("yl", "x")

    left = pl.pallas_call(
        left_gram_kernel, out_shape=f32(BLOCK, LANES), compiler_params=VMEM, name="left_gram"
    )(gradient)
    right = pl.pallas_call(
        right_gram_kernel, out_shape=f32(count, BLOCK, LANES), compiler_params=VMEM, name="right_gram"
    )(gradient)

    left = left + shift(left, "core", 1)
    left = left + shift(left, "z", 4)
    left = left + shift(left, "z", 2)
    left = left + shift(left, "z", 1)

    right = lax.all_to_all(right, group, 0, 0, tiled=True)
    right = jnp.sum(right, axis=0)
    right = lax.all_gather(right, "yh")
    root = pl.pallas_call(
        right_root_kernel,
        out_shape=f32(BLOCK, LANES),
        scratch_shapes=scratch,
        compiler_params=VMEM,
        name="right_root",
        cost_estimate=estimate(8 * 10**9),
    )(right)
    roots = copies(root, group, count)

    mid = pl.pallas_call(
        left_root_kernel,
        out_shape=f32(height, width),
        scratch_shapes=scratch,
        compiler_params=VMEM,
        name="left_root",
        cost_estimate=estimate(8 * 10**9),
    )(left, gradient)
    return pl.pallas_call(
        update_kernel, out_shape=f32(height, width), compiler_params=VMEM, name="update"
    )(mid, roots)


def solution(mesh):
    names = ("yh", "yl", "x", "z", "core")
    fine = Mesh(mesh.devices.reshape(4, 2, 4, 8, 2), names)
    spec = P(names[:3], names[3:])
    return jax.shard_map(body, mesh=fine, in_specs=(spec,), out_specs=spec, check_vma=False)
```

time: 1740 us -> 105 us (0.06)
  the two profiles are of different devices: /device:TPU:16 before, /device:TPU:6 now
where the time goes in v1:
time: 105 us
  blocking collectives  32.6 us (31%)
  starting transfers between devices  27.7 us (26%)
  Pallas kernels  24.4 us (23%)
  waiting for transfers between devices  17.6 us (17%)
  local copies, waits for them, and re-layouts  2.21 us (2%)
    ppermute x4, starting transfers between devices, shift(): return lax.ppermute(x, axis, [(i, (i + by) % n) for i in range(n)])  21.2 us
    ppermute x4, waiting for transfers between devices, shift(): return lax.ppermute(x, axis, [(i, (i + by) % n) for i in range(n)])  17.6 us
    all_gather x1, blocking collectives, body(): right = lax.all_gather(right, 'yh')  16.6 us
    all_to_all x1, blocking collectives, body(): right = lax.all_to_all(right, group, 0, 0, tiled=True)  16 us
    pallas_call x1, Pallas kernels, body(): pl.pallas_call(left_root_kernel, out_shape=f32(height, width), scratch_sh...  10.2 us
    pallas_call x1, Pallas kernels, body(): pl.pallas_call(right_root_kernel, out_shape=f32(BLOCK, LANES), scratch_sh...  9.54 us
    all_to_all x1, starting transfers between devices, copies(): lax.all_to_all(jnp.broadcast_to(x[None], (n,) + x.shape), axes, 0, 0, til...  6.54 us
    pallas_call x1, Pallas kernels, body(): pl.pallas_call(update_kernel, out_shape=f32(height, width), compiler_para...  2.86 us
  transfers between devices with their start and end apart: 5, of which 4 were waited for; matrix products, arithmetic and copies ran while one was open for 0% of the time, Pallas kernels for 10%

profile of v1, /device:TPU:6, one launch (start us, length us, event | category | flops | bytes accessed | tf_op | source)
XLA Modules:
  0.0 104.8 jit_solution(6507918186405118709)
XLA Ops:
  0.0 0.0 copy-start
  0.0 1.3 %copy-done = f32[192,1536]{1,0:T(8,128)S(1)} copy-done((f32[192,1536]{1,0:T(8,128)S(1)}, f32[192,1536]{1,0:T(8,128)}, u32[]{:S(2)}) %copy-start) | copy-done | bytes 1179672
  1.3 1.2 %right_gram.1 = f32[8,192,128]{2,1,0:T(8,128)S(1)} custom-call(f32[192,1536]{1,0:T(8,128)S(1)} %copy-done), custom_call_target="tpu_custom_call" | custom-call | tf_op jit(solution)/shard_map/right_gram/pallas_call | solution.py:140
  2.4 16.0 %all_to_all.10 = f32[8,192,128]{2,1,0:T(8,128)S(1)} all-to-all(f32[8,192,128]{2,1,0:T(8,128)S(1)} %right_gram.1), channel_id=1, replica_groups=mesh['yh'=4,'yl'=2,'x'=4,'z'=8,'core'=2] {'yl','x'}, dimensions={0} | all-to-all | bytes 1572864 | tf_op jit(solution)/shard_map/all_to_all | solution.py:149
  18.5 16.6 %all-gather = f32[768,128]{1,0:T(8,128)S(1)} all-gather(f32[192,128]{1,0:T(8,128)S(1)} %reduce_sum.9), channel_id=2, replica_groups=mesh['yh'=4,'yl'=2,'x'=4,'z'=8,'core'=2] {'yh'}, dimensions={0}, use_global_device_ids=true | all-gather | bytes 491520 | tf_op jit(solution)/shard_map/all_gather | solution.py:151
  35.1 9.5 %right_root.1 = f32[192,128]{1,0:T(8,128)S(1)} custom-call(f32[4,192,128]{2,1,0:T(8,128)S(1)} %bitcast.1), custom_call_target="tpu_custom_call" | custom-call | flops 8000000000 | bytes 1048576 | tf_op jit(solution)/shard_map/right_root/pallas_call | solution.py:152
  44.6 0.0 copy-start.1
  44.6 0.9 broadcast_in_dim.2
  45.6 6.5 %all-to-all-start.1 = ((f32[8,192,128]{2,1,0:T(8,128)}), f32[8,192,128]{2,1,0:T(8,128)S(1)}, u32[]{:S(2)}, u32[]{:S(2)}) async-start(f32[8,192,128]{2,1,0:T(8,128)} %broadcast_in_dim.2), calls=%async_computation.1 | async-start | bytes 1572864 | tf_op jit(solution)/shard_map/all_to_all | solution.py:128
  52.1 0.0 copy-done.1
  52.1 0.7 left_gram.1
  52.8 1.9 %collective-permute-start = (f32[192,128]{1,0:T(8,128)S(1)}, f32[192,128]{1,0:T(8,128)S(1)}, u32[]{:S(2)}, u32[]{:S(2)}) collective-permute-start(f32[192,128]{1,0:T(8,128)S(1)} %left_gram.1), channel_id=1, source_target_pairs={{0,1},{1,0},{2,3},{3,2},{4,5},{5,4},{6,7},{7,6},{8,9},{9,8},{10,11... | collective-permute-start | bytes 294920 | tf_op jit(solution)/shard_map/ppermute | solution.py:124
  54.7 1.3 %collective-permute-done = f32[192,128]{1,0:T(8,128)S(1)} collective-permute-done((f32[192,128]{1,0:T(8,128)S(1)}, f32[192,128]{1,0:T(8,128)S(1)}, u32[]{:S(2)}, u32[]{:S(2)}) %collective-permute-start) | collective-permute-done | bytes 98336 | tf_op jit(solution)/shard_map/ppermute | solution.py:124
  56.0 10.9 %collective-permute-start.1 = (f32[192,128]{1,0:T(8,128)S(1)}, f32[192,128]{1,0:T(8,128)S(1)}, u32[]{:S(2)}, u32[]{:S(2)}) collective-permute-start(f32[192,128]{1,0:T(8,128)S(1)} %add.12), channel_id=1, source_target_pairs={{0,8},{2,10},{4,12},{6,14},{8,0},{10,2},{12,4},{14,6},{1,9},{3,11}... | collective-permute-start | bytes 294920 | tf_op jit(solution)/shard_map/ppermute | solution.py:124
  67.0 3.2 %collective-permute-done.1 = f32[192,128]{1,0:T(8,128)S(1)} collective-permute-done((f32[192,128]{1,0:T(8,128)S(1)}, f32[192,128]{1,0:T(8,128)S(1)}, u32[]{:S(2)}, u32[]{:S(2)}) %collective-permute-start.1) | collective-permute-done | bytes 98336 | tf_op jit(solution)/shard_map/ppermute | solution.py:124
  70.2 6.4 %collective-permute-start.2 = (f32[192,128]{1,0:T(8,128)S(1)}, f32[192,128]{1,0:T(8,128)S(1)}, u32[]{:S(2)}, u32[]{:S(2)}) collective-permute-start(f32[192,128]{1,0:T(8,128)S(1)} %add.13), channel_id=1, source_target_pairs={{0,4},{2,6},{4,8},{6,10},{8,12},{10,14},{12,0},{14,2},{1,5},{3,7},... | collective-permute-start | bytes 294920 | tf_op jit(solution)/shard_map/ppermute | solution.py:124
  76.6 7.4 %collective-permute-done.2 = f32[192,128]{1,0:T(8,128)S(1)} collective-permute-done((f32[192,128]{1,0:T(8,128)S(1)}, f32[192,128]{1,0:T(8,128)S(1)}, u32[]{:S(2)}, u32[]{:S(2)}) %collective-permute-start.2) | collective-permute-done | bytes 98336 | tf_op jit(solution)/shard_map/ppermute | solution.py:124
  84.0 1.9 %collective-permute-start.3 = (f32[192,128]{1,0:T(8,128)S(1)}, f32[192,128]{1,0:T(8,128)S(1)}, u32[]{:S(2)}, u32[]{:S(2)}) collective-permute-start(f32[192,128]{1,0:T(8,128)S(1)} %add.14), channel_id=1, source_target_pairs={{0,2},{2,4},{4,6},{6,8},{8,10},{10,12},{12,14},{14,0},{1,3},{3,5},... | collective-permute-start | bytes 294920 | tf_op jit(solution)/shard_map/ppermute | solution.py:124
  85.9 5.8 %collective-permute-done.3 = f32[192,128]{1,0:T(8,128)S(1)} collective-permute-done((f32[192,128]{1,0:T(8,128)S(1)}, f32[192,128]{1,0:T(8,128)S(1)}, u32[]{:S(2)}, u32[]{:S(2)}) %collective-permute-start.3) | collective-permute-done | bytes 98336 | tf_op jit(solution)/shard_map/ppermute | solution.py:124
  91.7 10.2 %left_root.1.mid_ref = f32[192,1536]{1,0:T(8,128)S(1)} custom-call(f32[192,128]{1,0:T(8,128)S(1)} %add.15.gram_ref, f32[192,1536]{1,0:T(8,128)S(1)} %copy-done.1), custom_call_target="tpu_custom_call" | custom-call | flops 8000000000 | bytes 1048576 | tf_op jit(solution)/shard_map/left_root/pallas_call | solution.py:162
  101.9 0.0 all-to-all-done.1.roots_ref
  101.9 2.9 %update.1 = f32[192,1536]{1,0:T(8,128)} custom-call(f32[192,1536]{1,0:T(8,128)S(1)} %left_root.1.mid_ref, f32[8,192,128]{2,1,0:T(8,128)S(1)} %all-to-all-done.1.roots_ref), custom_call_target="tpu_custom_call" | custom-call | tf_op jit(solution)/shard_map/update/pallas_call | solution.py:170
  (5 shorter events, 0.1 us)
Async XLA Ops:
  0.0 1.3 %copy-start = (f32[192,1536]{1,0:T(8,128)S(1)}, f32[192,1536]{1,0:T(8,128)}, u32[]{:S(2)}) copy-start(f32[192,1536]{1,0:T(8,128)} %grad_ref.5) | copy-start | bytes 3538948
  44.6 7.5 %copy-start.1 = (f32[192,1536]{1,0:T(8,128)S(1)}, f32[192,1536]{1,0:T(8,128)}, u32[]{:S(2)}) copy-start(f32[192,1536]{1,0:T(8,128)} %grad_ref.5) | copy-start | bytes 3538948
  45.6 56.3 %all-to-all-start.1 = ((f32[8,192,128]{2,1,0:T(8,128)}), f32[8,192,128]{2,1,0:T(8,128)S(1)}, u32[]{:S(2)}, u32[]{:S(2)}) async-start(f32[8,192,128]{2,1,0:T(8,128)} %broadcast_in_dim.2), calls=%async_computation.1 | async-start | bytes 1572864 | tf_op jit(solution)/shard_map/all_to_all | solution.py:128
  52.8 3.2 %collective-permute-start = (f32[192,128]{1,0:T(8,128)S(1)}, f32[192,128]{1,0:T(8,128)S(1)}, u32[]{:S(2)}, u32[]{:S(2)}) collective-permute-start(f32[192,128]{1,0:T(8,128)S(1)} %left_gram.1), channel_id=1, source_target_pairs={{0,1},{1,0},{2,3},{3,2},{4,5},{5,4},{6,7},{7,6},{8,9},{9,8},{10,11... | collective-permute-start | bytes 294920 | tf_op jit(solution)/shard_map/ppermute | solution.py:124
  56.0 14.1 %collective-permute-start.1 = (f32[192,128]{1,0:T(8,128)S(1)}, f32[192,128]{1,0:T(8,128)S(1)}, u32[]{:S(2)}, u32[]{:S(2)}) collective-permute-start(f32[192,128]{1,0:T(8,128)S(1)} %add.12), channel_id=1, source_target_pairs={{0,8},{2,10},{4,12},{6,14},{8,0},{10,2},{12,4},{14,6},{1,9},{3,11}... | collective-permute-start | bytes 294920 | tf_op jit(solution)/shard_map/ppermute | solution.py:124
  70.2 13.8 %collective-permute-start.2 = (f32[192,128]{1,0:T(8,128)S(1)}, f32[192,128]{1,0:T(8,128)S(1)}, u32[]{:S(2)}, u32[]{:S(2)}) collective-permute-start(f32[192,128]{1,0:T(8,128)S(1)} %add.13), channel_id=1, source_target_pairs={{0,4},{2,6},{4,8},{6,10},{8,12},{10,14},{12,0},{14,2},{1,5},{3,7},... | collective-permute-start | bytes 294920 | tf_op jit(solution)/shard_map/ppermute | solution.py:124
  84.0 7.7 %collective-permute-start.3 = (f32[192,128]{1,0:T(8,128)S(1)}, f32[192,128]{1,0:T(8,128)S(1)}, u32[]{:S(2)}, u32[]{:S(2)}) collective-permute-start(f32[192,128]{1,0:T(8,128)S(1)} %add.14), channel_id=1, source_target_pairs={{0,2},{2,4},{4,6},{6,8},{8,10},{10,12},{12,14},{14,0},{1,3},{3,5},... | collective-permute-start | bytes 294920 | tf_op jit(solution)/shard_map/ppermute | solution.py:124

commit v2 on v1

v2 whole, which is shorter than its diff:
```python
import functools

import jax
import jax.numpy as jnp
from jax import lax
from jax.experimental import pallas as pl
from jax.experimental.pallas import tpu as pltpu
from jax.sharding import Mesh, PartitionSpec as P

D_IN = 6144
D_OUT = 24576
BLOCK = 192
ITERS = 12
HALF = 96
LANES = 128
PACKED = 152
CHUNK = 2 * BLOCK
SCALE = (float(D_IN) * float(D_OUT)) ** 0.25
F32, BF16 = jnp.float32, jnp.bfloat16
PARAMS = pltpu.CompilerParams(vmem_limit_bytes=32 * 2**20)


def split(a):
    high = a.astype(BF16)
    return high, (a - high.astype(F32)).astype(BF16)


def dot(a, b, dims=((1,), (0,))):
    return lax.dot_general(a, b, (dims, ((), ())), preferred_element_type=F32)


def product(a, b, dims=((1,), (0,))):
    return dot(a[0], b[0], dims) + (dot(a[0], b[1], dims) + dot(a[1], b[0], dims))


def grid_of(height, width):
    shape = (height, width)
    return lax.broadcasted_iota(jnp.int32, shape, 0), lax.broadcasted_iota(jnp.int32, shape, 1)


def pack(a):
    tail = a[HALF:, HALF:]
    row, col = grid_of(HALF, LANES)
    wide = jnp.concatenate([tail, jnp.zeros((HALF, LANES - HALF), F32)], axis=1)
    top = jnp.where(col < row, wide, a[:HALF, :LANES])
    rest = a[:HALF, LANES:]
    diagonal = jnp.sum(jnp.where(row == col, wide, 0.0), axis=0, keepdims=True)
    return jnp.concatenate(
        [
            top,
            jnp.concatenate([rest[: HALF // 2], rest[HALF // 2 :]], axis=1),
            jnp.broadcast_to(diagonal, (8, LANES)),
        ],
        axis=0,
    )


def unpack(p):
    row, col = grid_of(HALF, HALF)
    upper = p[:HALF, :HALF]
    lower = upper.T
    middle = p[HALF : HALF + HALF // 2]
    rest = jnp.concatenate(
        [p[:HALF, HALF:], jnp.concatenate([middle[:, :64], middle[:, 64:]], axis=0)], axis=1
    )
    head = jnp.where(col < row, lower, upper)
    tail = jnp.where(col < row, upper, jnp.where(col == row, p[144:145, :HALF], lower))
    return jnp.concatenate(
        [jnp.concatenate([head, rest], axis=1), jnp.concatenate([rest.T, tail], axis=1)], axis=0
    )


def gram_kernel(grad_ref, left_ref, right_ref):
    rows, columns = ((0,), (0,)), ((1,), (1,))
    left = None
    for k in range(grad_ref.shape[1] // CHUNK):
        g = split(grad_ref[:, k * CHUNK : (k + 1) * CHUNK])
        part = product(g, g, columns)
        left = part if k == 0 else left + part
        for c in range(CHUNK // BLOCK):
            h = [part[:, c * BLOCK : (c + 1) * BLOCK] for part in g]
            right_ref[k * (CHUNK // BLOCK) + c] = pack(product(h, h, rows))
    left_ref[...] = pack(left)


def newton(gram, m_ref, x_ref):
    row, col = grid_of(BLOCK, BLOCK)
    identity = (row == col).astype(F32)
    damped = gram + (0.01 / BLOCK * jnp.sum(gram * identity)) * identity
    norm = jnp.sqrt(jnp.sum(damped * damped, keepdims=True))
    m = damped / norm
    bands = [slice(0, HALF), slice(HALF, BLOCK)]

    def advance(m):
        parts = split(m)
        squares = [
            split(
                (25.0 * identity[b] - 10.0 * m[b] + product((parts[0][b], parts[1][b]), parts))
                * 0.0625
            )
            for b in bands
        ]
        halfway = [split(product(s, parts)) for s in squares]
        square = [jnp.concatenate([s[k] for s in squares], axis=0) for k in range(2)]
        return parts, jnp.concatenate([product(h, square) for h in halfway], axis=0)

    def grow(parts):
        x = x_ref[...]
        return jnp.concatenate(
            [1.25 * x[b] - 0.25 * product(split(x[b]), parts) for b in bands], axis=0
        )

    x_ref[...] = (5.0 * identity - m) * 0.25
    m_ref[...] = advance(m)[1]

    def step(k, carry):
        parts, following = advance(m_ref[...])
        m_ref[...] = following
        x_ref[...] = grow(parts)
        return carry

    lax.fori_loop(0, ITERS - 2, step, 0, unroll=5)
    return grow(split(m_ref[...])) * lax.rsqrt(jnp.sqrt(norm))


def right_root_kernel(*refs):
    *parts, roots_ref, m_ref, x_ref = refs
    total = functools.reduce(lambda a, b: a + b, [ref[...] for ref in parts])
    root = pack(newton(unpack(total), m_ref, x_ref))
    for k in range(roots_ref.shape[0]):
        roots_ref[k] = root


def left_root_kernel(gram_ref, grad_ref, high_ref, low_ref, m_ref, x_ref):
    root = split(newton(unpack(gram_ref[...]), m_ref, x_ref))
    for k in range(grad_ref.shape[1] // CHUNK):
        mid = split(product(root, split(grad_ref[:, k * CHUNK : (k + 1) * CHUNK])))
        for c in range(CHUNK // BLOCK):
            window = slice(c * BLOCK, (c + 1) * BLOCK)
            high_ref[2 * k + c] = mid[0][:, window]
            low_ref[2 * k + c] = mid[1][:, window]


def update_kernel(high_ref, low_ref, roots_ref, out_ref, held, sems):
    stores = []
    for k in range(out_ref.shape[1] // CHUNK):
        for c in range(CHUNK // BLOCK):
            b = 2 * k + c
            root = split(unpack(roots_ref[b]))
            held[k, :, c * BLOCK : (c + 1) * BLOCK] = product((high_ref[b], low_ref[b]), root) * SCALE
        stores.append(
            pltpu.make_async_copy(held.at[k], out_ref.at[:, pl.ds(k * CHUNK, CHUNK)], sems.at[k])
        )
        stores[-1].start()
    for store in stores:
        store.wait()


def shape(*dims, dtype=F32):
    return jax.ShapeDtypeStruct(dims, dtype)


def estimate(flops):
    return pl.CostEstimate(flops=flops, bytes_accessed=2**20, transcendentals=0)


def shift(x, axis, by):
    n = lax.axis_size(axis)
    return lax.ppermute(x, axis, [(i, (i + by) % n) for i in range(n)])


def swap(x, axes):
    return lax.all_to_all(x, axes, 0, 0, tiled=True)


def body(gradient):
    height, width = gradient.shape
    count = width // BLOCK
    chunks = width // CHUNK
    group = ("yl", "x")
    line = ("zl", "core")
    ranks = lax.axis_size(line)
    square = [pltpu.VMEM((BLOCK, BLOCK), F32)] * 2
    whole = [pltpu.VMEM((chunks, height, CHUNK), F32), pltpu.SemaphoreType.DMA((chunks,))]

    left, right = pl.pallas_call(
        gram_kernel,
        out_shape=[shape(PACKED, LANES), shape(count, PACKED, LANES)],
        compiler_params=PARAMS,
        name="grams",
    )(gradient)
    right = swap(right, group)
    left = left + shift(left, "zh", 1)
    right, left = lax.optimization_barrier((jnp.sum(right, axis=0), left))
    rest = [right] + [shift(right, "yh", by) for by in (3, 1, 2)]
    left = jnp.sum(swap(jnp.broadcast_to(left[None], (ranks,) + left.shape), line), axis=0)

    roots = pl.pallas_call(
        right_root_kernel,
        out_shape=shape(count, PACKED, LANES),
        scratch_shapes=square,
        compiler_params=PARAMS,
        name="right_root",
        cost_estimate=estimate(16 * 10**9),
    )(*rest)
    roots, left = lax.optimization_barrier((roots, left))
    received = swap(roots, group)

    high, low = pl.pallas_call(
        left_root_kernel,
        out_shape=[shape(count, height, BLOCK, dtype=BF16)] * 2,
        scratch_shapes=square,
        compiler_params=PARAMS,
        name="left_root",
        cost_estimate=estimate(8 * 10**9),
    )(left, gradient)
    return pl.pallas_call(
        update_kernel,
        out_specs=pl.BlockSpec(memory_space=pl.ANY),
        out_shape=shape(height, width),
        scratch_shapes=whole,
        compiler_params=PARAMS,
        name="update",
    )(high, low, received)


def solution(mesh):
    names = ("yh", "yl", "x", "zh", "zl", "core")
    fine = Mesh(mesh.devices.reshape(4, 2, 4, 2, 4, 2), names)
    spec = P(names[:3], names[3:])
    return jax.shard_map(body, mesh=fine, in_specs=(spec,), out_specs=spec, check_vma=False)
```

time: 105 us -> 79.2 us (0.75)
  the two profiles are of different devices: /device:TPU:6 before, /device:TPU:8 now
where the time goes in v2:
time: 79.2 us; the launch traced here: 78.8 us
  starting transfers between devices  41.4 us (52%)
  Pallas kernels  23 us (29%)
  waiting for transfers between devices  12 us (15%)
  local copies, waits for them, and re-layouts  2.14 us (3%)
    ppermute x4, starting transfers between devices, shift(): return lax.ppermute(x, axis, [(i, (i + by) % n) for i in range(n)])  22.2 us
    all_to_all x3, starting transfers between devices, swap(): return lax.all_to_all(x, axes, 0, 0, tiled=True)  19.3 us
    all_to_all x3, waiting for transfers between devices, swap(): return lax.all_to_all(x, axes, 0, 0, tiled=True)  9.12 us
    pallas_call x1, Pallas kernels, body(): pl.pallas_call(right_root_kernel, out_shape=shape(count, PACKED, LANES),...  8.96 us
    pallas_call x1, Pallas kernels, body(): pl.pallas_call(left_root_kernel, out_shape=[shape(count, height, BLOCK, d...  8.83 us
    ppermute x4, waiting for transfers between devices, shift(): return lax.ppermute(x, axis, [(i, (i + by) % n) for i in range(n)])  2.91 us
    pallas_call x1, Pallas kernels, body(): pl.pallas_call(update_kernel, out_specs=pl.BlockSpec(memory_space=pl.ANY)...  2.81 us
    pallas_call x1, Pallas kernels, body(): pl.pallas_call(gram_kernel, out_shape=[shape(PACKED, LANES), shape(count,...  2.36 us
  transfers between devices with their start and end apart: 7, of which 3 were waited for; matrix products, arithmetic and copies ran while one was open for 1% of the time, Pallas kernels for 23%

profile of v2, /device:TPU:8, one launch (start us, length us, event | category | flops | bytes accessed | tf_op | source)
XLA Modules:
  0.0 78.8 jit_solution(7307913402417461038)
XLA Ops:
  0.0 0.0 copy-start
  0.0 1.3 %copy-done = f32[192,1536]{1,0:T(8,128)S(1)} copy-done((f32[192,1536]{1,0:T(8,128)S(1)}, f32[192,1536]{1,0:T(8,128)}, u32[]{:S(2)}) %copy-start) | copy-done | bytes 1179672
  1.3 2.4 %grams.1 = (f32[152,128]{1,0:T(8,128)S(1)}, f32[8,152,128]{2,1,0:T(8,128)}) custom-call(f32[192,1536]{1,0:T(8,128)S(1)} %copy-done), custom_call_target="tpu_custom_call" | custom-call | tf_op jit(solution)/shard_map/grams/pallas_call | solution.py:186
  3.6 9.3 %all-to-all-start = ((f32[8,152,128]{2,1,0:T(8,128)}), f32[8,152,128]{2,1,0:T(8,128)S(1)}, u32[]{:S(2)}, u32[]{:S(2)}) async-start(f32[8,152,128]{2,1,0:T(8,128)} %get-tuple-element.13), calls=%async_computation | async-start | bytes 1245184 | tf_op jit(solution)/shard_map/all_to_all | solution.py:173
  12.9 7.4 %collective-permute-start = (f32[152,128]{1,0:T(8,128)S(1)}, f32[152,128]{1,0:T(8,128)S(1)}, u32[]{:S(2)}, u32[]{:S(2)}) collective-permute-start(f32[152,128]{1,0:T(8,128)S(1)} %get-tuple-element.14), channel_id=1, source_target_pairs={{0,8},{8,0},{1,9},{9,1},{2,10},{10,2},{3,11},{11,3},{4,12},{12,4},... | collective-permute-start | bytes 233480 | tf_op jit(solution)/shard_map/ppermute | solution.py:169
  20.3 2.9 %collective-permute-done = f32[152,128]{1,0:T(8,128)S(1)} collective-permute-done((f32[152,128]{1,0:T(8,128)S(1)}, f32[152,128]{1,0:T(8,128)S(1)}, u32[]{:S(2)}, u32[]{:S(2)}) %collective-permute-start) | collective-permute-done | bytes 77856 | tf_op jit(solution)/shard_map/ppermute | solution.py:169
  23.2 0.0 all-to-all-done
  23.3 6.8 %collective-permute-start.3 = (f32[152,128]{1,0:T(8,128)S(1)}, f32[152,128]{1,0:T(8,128)S(1)}, u32[]{:S(2)}, u32[]{:S(2)}) collective-permute-start(f32[152,128]{1,0:T(8,128)S(1)} %reduce_sum.18.refs_0_), channel_id=1, source_target_pairs={{0,256},{128,384},{256,0},{384,128},{1,257},{129,385},{257,1},{385... | collective-permute-start | bytes 233480 | tf_op jit(solution)/shard_map/ppermute | solution.py:169
  30.1 2.7 %collective-permute-start.2 = (f32[152,128]{1,0:T(8,128)S(1)}, f32[152,128]{1,0:T(8,128)S(1)}, u32[]{:S(2)}, u32[]{:S(2)}) collective-permute-start(f32[152,128]{1,0:T(8,128)S(1)} %reduce_sum.18.refs_0_), channel_id=1, source_target_pairs={{0,128},{128,256},{256,384},{384,0},{1,129},{129,257},{257,385},{3... | collective-permute-start | bytes 233480 | tf_op jit(solution)/shard_map/ppermute | solution.py:169
  32.8 5.3 %collective-permute-start.1 = (f32[152,128]{1,0:T(8,128)S(1)}, f32[152,128]{1,0:T(8,128)S(1)}, u32[]{:S(2)}, u32[]{:S(2)}) collective-permute-start(f32[152,128]{1,0:T(8,128)S(1)} %reduce_sum.18.refs_0_), channel_id=1, source_target_pairs={{0,384},{128,0},{256,128},{384,256},{1,385},{129,1},{257,129},{385... | collective-permute-start | bytes 233480 | tf_op jit(solution)/shard_map/ppermute | solution.py:169
  38.1 0.9 %broadcast_in_dim.2 = f32[8,152,128]{2,1,0:T(8,128)} broadcast(f32[152,128]{1,0:T(8,128)S(1)} %add.3), dimensions={1,2} | broadcast | bytes 700416 | tf_op jit(solution)/shard_map/broadcast_in_dim | solution.py:196
  39.0 4.3 %all-to-all-start.1 = ((f32[8,152,128]{2,1,0:T(8,128)}), f32[8,152,128]{2,1,0:T(8,128)S(1)}, u32[]{:S(2)}, u32[]{:S(2)}) async-start(f32[8,152,128]{2,1,0:T(8,128)} %broadcast_in_dim.2), calls=%async_computation.1 | async-start | bytes 1245184 | tf_op jit(solution)/shard_map/all_to_all | solution.py:173
  43.2 0.0 collective-permute-done.3.refs_3_
  43.2 0.0 collective-permute-done.2.refs_2_
  43.3 0.0 collective-permute-done.1.refs_1_
  43.3 9.0 %right_root.1 = f32[8,152,128]{2,1,0:T(8,128)} custom-call(f32[152,128]{1,0:T(8,128)S(1)} %reduce_sum.18.refs_0_, f32[152,128]{1,0:T(8,128)S(1)} %collective-permute-done.1.refs_1_, f32[152,128]{1,0:T(8,128)S(1)} %collective-permute-done.2.refs_2_, f32[152,128]{1,0:T(8,128)S(1)} %collective-permute-done.3.refs_3_), custom_call_target="tpu_custom_call" | custom-call | flops 16000000000 | bytes 1048576 | tf_op jit(solution)/shard_map/right_root/pallas_call | solution.py:198
  52.2 0.0 copy-start.1
  52.2 8.5 %all-to-all-done.1 = f32[8,152,128]{2,1,0:T(8,128)S(1)} async-done(((f32[8,152,128]{2,1,0:T(8,128)}), f32[8,152,128]{2,1,0:T(8,128)S(1)}, u32[]{:S(2)}, u32[]{:S(2)}) %all-to-all-start.1) | async-done | bytes 622624 | tf_op jit(solution)/shard_map/all_to_all | solution.py:173
  60.7 5.7 %all-to-all-start.2 = ((f32[8,152,128]{2,1,0:T(8,128)}), f32[8,152,128]{2,1,0:T(8,128)S(1)}, u32[]{:S(2)}, u32[]{:S(2)}) async-start(f32[8,152,128]{2,1,0:T(8,128)} %right_root.1), calls=%async_computation.2 | async-start | bytes 1245184 | tf_op jit(solution)/shard_map/all_to_all | solution.py:173
  66.5 0.0 copy-done.1
  66.5 8.8 %left_root.1 = (bf16[8,192,192]{2,1,0:T(8,128)(2,1)S(1)}, bf16[8,192,192]{2,1,0:T(8,128)(2,1)S(1)}) custom-call(f32[152,128]{1,0:T(8,128)S(1)} %reduce_sum.19.gram_ref, f32[192,1536]{1,0:T(8,128)S(1)} %copy-done.1), custom_call_target="tpu_custom_call" | custom-call | flops 8000000000 | bytes 1048576 | tf_op jit(solution)/shard_map/left_root/pallas_call | solution.py:209
  75.3 0.6 all-to-all-done.2.roots_ref
  75.9 2.8 %update.1 = f32[192,1536]{1,0:T(8,128)} custom-call(bf16[8,192,192]{2,1,0:T(8,128)(2,1)S(1)} %get-tuple-element.18.high_ref, bf16[8,192,192]{2,1,0:T(8,128)(2,1)S(1)} %get-tuple-element.19.low_ref, f32[8,152,128]{2,1,0:T(8,128)S(1)} %all-to-all-done.2.roots_ref), custom_call_target="tpu_custom_call" | custom-call | tf_op jit(solution)/shard_map/update/pallas_call | solution.py:217
  (3 shorter events, 0.1 us)
Async XLA Ops:
  0.0 1.3 %copy-start = (f32[192,1536]{1,0:T(8,128)S(1)}, f32[192,1536]{1,0:T(8,128)}, u32[]{:S(2)}) copy-start(f32[192,1536]{1,0:T(8,128)} %grad_ref.3) | copy-start | bytes 3538948
  3.6 19.6 %all-to-all-start = ((f32[8,152,128]{2,1,0:T(8,128)}), f32[8,152,128]{2,1,0:T(8,128)S(1)}, u32[]{:S(2)}, u32[]{:S(2)}) async-start(f32[8,152,128]{2,1,0:T(8,128)} %get-tuple-element.13), calls=%async_computation | async-start | bytes 1245184 | tf_op jit(solution)/shard_map/all_to_all | solution.py:173
  12.9 10.3 %collective-permute-start = (f32[152,128]{1,0:T(8,128)S(1)}, f32[152,128]{1,0:T(8,128)S(1)}, u32[]{:S(2)}, u32[]{:S(2)}) collective-permute-start(f32[152,128]{1,0:T(8,128)S(1)} %get-tuple-element.14), channel_id=1, source_target_pairs={{0,8},{8,0},{1,9},{9,1},{2,10},{10,2},{3,11},{11,3},{4,12},{12,4},... | collective-permute-start | bytes 233480 | tf_op jit(solution)/shard_map/ppermute | solution.py:169
  23.3 20.0 %collective-permute-start.3 = (f32[152,128]{1,0:T(8,128)S(1)}, f32[152,128]{1,0:T(8,128)S(1)}, u32[]{:S(2)}, u32[]{:S(2)}) collective-permute-start(f32[152,128]{1,0:T(8,128)S(1)} %reduce_sum.18.refs_0_), channel_id=1, source_target_pairs={{0,256},{128,384},{256,0},{384,128},{1,257},{129,385},{257,1},{385... | collective-permute-start | bytes 233480 | tf_op jit(solution)/shard_map/ppermute | solution.py:169
  30.1 13.1 %collective-permute-start.2 = (f32[152,128]{1,0:T(8,128)S(1)}, f32[152,128]{1,0:T(8,128)S(1)}, u32[]{:S(2)}, u32[]{:S(2)}) collective-permute-start(f32[152,128]{1,0:T(8,128)S(1)} %reduce_sum.18.refs_0_), channel_id=1, source_target_pairs={{0,128},{128,256},{256,384},{384,0},{1,129},{129,257},{257,385},{3... | collective-permute-start | bytes 233480 | tf_op jit(solution)/shard_map/ppermute | solution.py:169
  32.8 10.4 %collective-permute-start.1 = (f32[152,128]{1,0:T(8,128)S(1)}, f32[152,128]{1,0:T(8,128)S(1)}, u32[]{:S(2)}, u32[]{:S(2)}) collective-permute-start(f32[152,128]{1,0:T(8,128)S(1)} %reduce_sum.18.refs_0_), channel_id=1, source_target_pairs={{0,384},{128,0},{256,128},{384,256},{1,385},{129,1},{257,129},{385... | collective-permute-start | bytes 233480 | tf_op jit(solution)/shard_map/ppermute | solution.py:169
  39.0 21.7 %all-to-all-start.1 = ((f32[8,152,128]{2,1,0:T(8,128)}), f32[8,152,128]{2,1,0:T(8,128)S(1)}, u32[]{:S(2)}, u32[]{:S(2)}) async-start(f32[8,152,128]{2,1,0:T(8,128)} %broadcast_in_dim.2), calls=%async_computation.1 | async-start | bytes 1245184 | tf_op jit(solution)/shard_map/all_to_all | solution.py:173
  52.2 14.2 %copy-start.1 = (f32[192,1536]{1,0:T(8,128)S(1)}, f32[192,1536]{1,0:T(8,128)}, u32[]{:S(2)}) copy-start(f32[192,1536]{1,0:T(8,128)} %grad_ref.3) | copy-start | bytes 3538948
  60.7 15.2 %all-to-all-start.2 = ((f32[8,152,128]{2,1,0:T(8,128)}), f32[8,152,128]{2,1,0:T(8,128)S(1)}, u32[]{:S(2)}, u32[]{:S(2)}) async-start(f32[8,152,128]{2,1,0:T(8,128)} %right_root.1), calls=%async_computation.2 | async-start | bytes 1245184 | tf_op jit(solution)/shard_map/all_to_all | solution.py:173

commit v3 on v2

--- a/solution.py
+++ b/solution.py
@@ -123,9 +123,8 @@
     return grow(split(m_ref[...])) * lax.rsqrt(jnp.sqrt(norm))
 
 
-def right_root_kernel(*refs):
-    *parts, roots_ref, m_ref, x_ref = refs
-    total = functools.reduce(lambda a, b: a + b, [ref[...] for ref in parts])
+def right_root_kernel(parts_ref, roots_ref, m_ref, x_ref):
+    total = functools.reduce(lambda a, b: a + b, [parts_ref[k] for k in range(parts_ref.shape[0])])
     root = pack(newton(unpack(total), m_ref, x_ref))
     for k in range(roots_ref.shape[0]):
         roots_ref[k] = root
@@ -166,7 +165,7 @@
 
 def shift(x, axis, by):
     n = lax.axis_size(axis)
-    return lax.ppermute(x, axis, [(i, (i + by) % n) for i in range(n)])
+    return lax.ppermute(x, axis, [(i, i ^ 1 if by == 1 else (i + by) % n) for i in range(n)])
 
 
 def swap(x, axes):
@@ -178,8 +177,6 @@
     count = width // BLOCK
     chunks = width // CHUNK
     group = ("yl", "x")
-    line = ("zl", "core")
-    ranks = lax.axis_size(line)
     square = [pltpu.VMEM((BLOCK, BLOCK), F32)] * 2
     whole = [pltpu.VMEM((chunks, height, CHUNK), F32), pltpu.SemaphoreType.DMA((chunks,))]
 
@@ -190,10 +187,13 @@
         name="grams",
     )(gradient)
     right = swap(right, group)
-    left = left + shift(left, "zh", 1)
+    left = left + shift(left, "core", 1)
+    left = left + shift(left, "z", 1)
     right, left = lax.optimization_barrier((jnp.sum(right, axis=0), left))
-    rest = [right] + [shift(right, "yh", by) for by in (3, 1, 2)]
-    left = jnp.sum(swap(jnp.broadcast_to(left[None], (ranks,) + left.shape), line), axis=0)
+    rest = swap(jnp.broadcast_to(right[None], (lax.axis_size("yh"),) + right.shape), "yh")
+    left = left + shift(left, "z", 4)
+    rest, left = lax.optimization_barrier((rest, left))
+    left = left + shift(left, "z", 2)
 
     roots = pl.pallas_call(
         right_root_kernel,
@@ -202,7 +202,7 @@
         compiler_params=PARAMS,
         name="right_root",
         cost_estimate=estimate(16 * 10**9),
-    )(*rest)
+    )(rest)
     roots, left = lax.optimization_barrier((roots, left))
     received = swap(roots, group)
 
@@ -225,7 +225,7 @@
 
 
 def solution(mesh):
-    names = ("yh", "yl", "x", "zh", "zl", "core")
-    fine = Mesh(mesh.devices.reshape(4, 2, 4, 2, 4, 2), names)
+    names = ("yh", "yl", "x", "z", "core")
+    fine = Mesh(mesh.devices.reshape(4, 2, 4, 8, 2), names)
     spec = P(names[:3], names[3:])
     return jax.shard_map(body, mesh=fine, in_specs=(spec,), out_specs=spec, check_vma=False)

time: 79.2 us -> 72.3 us (0.913)
  the two profiles are of different devices: /device:TPU:8 before, /device:TPU:40 now
where the time goes in v3:
time: 72.3 us; the launch traced here: 71.8 us
  starting transfers between devices  40 us (55%)
  Pallas kernels  23 us (32%)
  waiting for transfers between devices  6.63 us (9%)
  local copies, waits for them, and re-layouts  2.01 us (3%)
    ppermute x4, starting transfers between devices, shift(): lax.ppermute(x, axis, [(i, i ^ 1 if by == 1 else (i + by) % n) for i in r...  21.4 us
    all_to_all x3, starting transfers between devices, swap(): return lax.all_to_all(x, axes, 0, 0, tiled=True)  18.6 us
    pallas_call x1, Pallas kernels, body(): pl.pallas_call(right_root_kernel, out_shape=shape(count, PACKED, LANES),...  8.95 us
    pallas_call x1, Pallas kernels, body(): pl.pallas_call(left_root_kernel, out_shape=[shape(count, height, BLOCK, d...  8.83 us
    ppermute x4, waiting for transfers between devices, shift(): lax.ppermute(x, axis, [(i, i ^ 1 if by == 1 else (i + by) % n) for i in r...  6.62 us
    pallas_call x1, Pallas kernels, body(): pl.pallas_call(update_kernel, out_specs=pl.BlockSpec(memory_space=pl.ANY)...  2.82 us
    pallas_call x1, Pallas kernels, body(): pl.pallas_call(gram_kernel, out_shape=[shape(PACKED, LANES), shape(count,...  2.36 us
  transfers between devices with their start and end apart: 7, of which 3 were waited for; matrix products, arithmetic and copies ran while one was open for 0% of the time, Pallas kernels for 25%

profile of v3, /device:TPU:40, one launch (start us, length us, event | category | flops | bytes accessed | tf_op | source)
XLA Modules:
  0.0 71.8 jit_solution(8073278576893480310)
XLA Ops:
  0.0 0.0 copy-start
  0.0 1.3 %copy-done = f32[192,1536]{1,0:T(8,128)S(1)} copy-done((f32[192,1536]{1,0:T(8,128)S(1)}, f32[192,1536]{1,0:T(8,128)}, u32[]{:S(2)}) %copy-start) | copy-done | bytes 1179672
  1.3 2.4 %grams.1 = (f32[152,128]{1,0:T(8,128)S(1)}, f32[8,152,128]{2,1,0:T(8,128)}) custom-call(f32[192,1536]{1,0:T(8,128)S(1)} %copy-done), custom_call_target="tpu_custom_call" | custom-call | tf_op jit(solution)/shard_map/grams/pallas_call | solution.py:183
  3.6 5.8 %all-to-all-start = ((f32[8,152,128]{2,1,0:T(8,128)}), f32[8,152,128]{2,1,0:T(8,128)S(1)}, u32[]{:S(2)}, u32[]{:S(2)}) async-start(f32[8,152,128]{2,1,0:T(8,128)} %get-tuple-element.15), calls=%async_computation | async-start | bytes 1245184 | tf_op jit(solution)/shard_map/all_to_all | solution.py:172
  9.4 1.9 %collective-permute-start = (f32[152,128]{1,0:T(8,128)S(1)}, f32[152,128]{1,0:T(8,128)S(1)}, u32[]{:S(2)}, u32[]{:S(2)}) collective-permute-start(f32[152,128]{1,0:T(8,128)S(1)} %get-tuple-element.16), channel_id=1, source_target_pairs={{0,1},{1,0},{2,3},{3,2},{4,5},{5,4},{6,7},{7,6},{8,9},{9,8},{10,11... | collective-permute-start | bytes 233480 | tf_op jit(solution)/shard_map/ppermute | solution.py:168
  11.3 1.2 %collective-permute-done = f32[152,128]{1,0:T(8,128)S(1)} collective-permute-done((f32[152,128]{1,0:T(8,128)S(1)}, f32[152,128]{1,0:T(8,128)S(1)}, u32[]{:S(2)}, u32[]{:S(2)}) %collective-permute-start) | collective-permute-done | bytes 77856 | tf_op jit(solution)/shard_map/ppermute | solution.py:168
  12.6 4.3 %collective-permute-start.1 = (f32[152,128]{1,0:T(8,128)S(1)}, f32[152,128]{1,0:T(8,128)S(1)}, u32[]{:S(2)}, u32[]{:S(2)}) collective-permute-start(f32[152,128]{1,0:T(8,128)S(1)} %add.12), channel_id=1, source_target_pairs={{0,2},{2,0},{4,6},{6,4},{8,10},{10,8},{12,14},{14,12},{1,3},{3,1},... | collective-permute-start | bytes 233480 | tf_op jit(solution)/shard_map/ppermute | solution.py:168
  16.8 2.7 %collective-permute-done.1 = f32[152,128]{1,0:T(8,128)S(1)} collective-permute-done((f32[152,128]{1,0:T(8,128)S(1)}, f32[152,128]{1,0:T(8,128)S(1)}, u32[]{:S(2)}, u32[]{:S(2)}) %collective-permute-start.1) | collective-permute-done | bytes 77856 | tf_op jit(solution)/shard_map/ppermute | solution.py:168
  19.5 0.0 all-to-all-done
  19.6 0.7 %broadcast_in_dim.2 = f32[4,152,128]{2,1,0:T(8,128)} broadcast(f32[152,128]{1,0:T(8,128)S(1)} %reduce_sum.9), dimensions={1,2} | broadcast | bytes 389120 | tf_op jit(solution)/shard_map/broadcast_in_dim | solution.py:193
  20.3 7.3 %all-to-all-start.1 = ((f32[4,152,128]{2,1,0:T(8,128)}), f32[4,152,128]{2,1,0:T(8,128)S(1)}, u32[]{:S(2)}, u32[]{:S(2)}) async-start(f32[4,152,128]{2,1,0:T(8,128)} %broadcast_in_dim.2), calls=%async_computation.1 | async-start | bytes 622592 | tf_op jit(solution)/shard_map/all_to_all | solution.py:172
  27.6 10.3 %collective-permute-start.2 = (f32[152,128]{1,0:T(8,128)S(1)}, f32[152,128]{1,0:T(8,128)S(1)}, u32[]{:S(2)}, u32[]{:S(2)}) collective-permute-start(f32[152,128]{1,0:T(8,128)S(1)} %add.13), channel_id=1, source_target_pairs={{0,8},{2,10},{4,12},{6,14},{8,0},{10,2},{12,4},{14,6},{1,9},{3,11}... | collective-permute-start | bytes 233480 | tf_op jit(solution)/shard_map/ppermute | solution.py:168
  38.0 2.7 %collective-permute-done.2 = f32[152,128]{1,0:T(8,128)S(1)} collective-permute-done((f32[152,128]{1,0:T(8,128)S(1)}, f32[152,128]{1,0:T(8,128)S(1)}, u32[]{:S(2)}, u32[]{:S(2)}) %collective-permute-start.2) | collective-permute-done | bytes 77856 | tf_op jit(solution)/shard_map/ppermute | solution.py:168
  40.7 0.0 all-to-all-done.1.parts_ref
  40.7 4.9 %collective-permute-start.3 = (f32[152,128]{1,0:T(8,128)S(1)}, f32[152,128]{1,0:T(8,128)S(1)}, u32[]{:S(2)}, u32[]{:S(2)}) collective-permute-start(f32[152,128]{1,0:T(8,128)S(1)} %add.14), channel_id=1, source_target_pairs={{0,4},{2,6},{4,8},{6,10},{8,12},{10,14},{12,0},{14,2},{1,5},{3,7},... | collective-permute-start | bytes 233480 | tf_op jit(solution)/shard_map/ppermute | solution.py:168
  45.6 8.9 %right_root.1 = f32[8,152,128]{2,1,0:T(8,128)} custom-call(f32[4,152,128]{2,1,0:T(8,128)S(1)} %all-to-all-done.1.parts_ref), custom_call_target="tpu_custom_call" | custom-call | flops 16000000000 | bytes 1048576 | tf_op jit(solution)/shard_map/right_root/pallas_call | solution.py:198
  54.6 0.0 copy-start.1
  54.6 0.0 collective-permute-done.3
  54.6 5.5 %all-to-all-start.2 = ((f32[8,152,128]{2,1,0:T(8,128)}), f32[8,152,128]{2,1,0:T(8,128)S(1)}, u32[]{:S(2)}, u32[]{:S(2)}) async-start(f32[8,152,128]{2,1,0:T(8,128)} %right_root.1), calls=%async_computation.2 | async-start | bytes 1245184 | tf_op jit(solution)/shard_map/all_to_all | solution.py:172
  60.1 0.0 copy-done.1
  60.1 8.8 %left_root.1 = (bf16[8,192,192]{2,1,0:T(8,128)(2,1)S(1)}, bf16[8,192,192]{2,1,0:T(8,128)(2,1)S(1)}) custom-call(f32[152,128]{1,0:T(8,128)S(1)} %add.15.gram_ref, f32[192,1536]{1,0:T(8,128)S(1)} %copy-done.1), custom_call_target="tpu_custom_call" | custom-call | flops 8000000000 | bytes 1048576 | tf_op jit(solution)/shard_map/left_root/pallas_call | solution.py:209
  69.0 0.0 all-to-all-done.2.roots_ref
  69.0 2.8 %update.1 = f32[192,1536]{1,0:T(8,128)} custom-call(bf16[8,192,192]{2,1,0:T(8,128)(2,1)S(1)} %get-tuple-element.22.high_ref, bf16[8,192,192]{2,1,0:T(8,128)(2,1)S(1)} %get-tuple-element.23.low_ref, f32[8,152,128]{2,1,0:T(8,128)S(1)} %all-to-all-done.2.roots_ref), custom_call_target="tpu_custom_call" | custom-call | tf_op jit(solution)/shard_map/update/pallas_call | solution.py:217
  (5 shorter events, 0.1 us)
Async XLA Ops:
  0.0 1.3 %copy-start = (f32[192,1536]{1,0:T(8,128)S(1)}, f32[192,1536]{1,0:T(8,128)}, u32[]{:S(2)}) copy-start(f32[192,1536]{1,0:T(8,128)} %grad_ref.3) | copy-start | bytes 3538948
  3.6 15.9 %all-to-all-start = ((f32[8,152,128]{2,1,0:T(8,128)}), f32[8,152,128]{2,1,0:T(8,128)S(1)}, u32[]{:S(2)}, u32[]{:S(2)}) async-start(f32[8,152,128]{2,1,0:T(8,128)} %get-tuple-element.15), calls=%async_computation | async-start | bytes 1245184 | tf_op jit(solution)/shard_map/all_to_all | solution.py:172
  9.4 3.2 %collective-permute-start = (f32[152,128]{1,0:T(8,128)S(1)}, f32[152,128]{1,0:T(8,128)S(1)}, u32[]{:S(2)}, u32[]{:S(2)}) collective-permute-start(f32[152,128]{1,0:T(8,128)S(1)} %get-tuple-element.16), channel_id=1, source_target_pairs={{0,1},{1,0},{2,3},{3,2},{4,5},{5,4},{6,7},{7,6},{8,9},{9,8},{10,11... | collective-permute-start | bytes 233480 | tf_op jit(solution)/shard_map/ppermute | solution.py:168
  12.6 6.9 %collective-permute-start.1 = (f32[152,128]{1,0:T(8,128)S(1)}, f32[152,128]{1,0:T(8,128)S(1)}, u32[]{:S(2)}, u32[]{:S(2)}) collective-permute-start(f32[152,128]{1,0:T(8,128)S(1)} %add.12), channel_id=1, source_target_pairs={{0,2},{2,0},{4,6},{6,4},{8,10},{10,8},{12,14},{14,12},{1,3},{3,1},... | collective-permute-start | bytes 233480 | tf_op jit(solution)/shard_map/ppermute | solution.py:168
  20.3 20.4 %all-to-all-start.1 = ((f32[4,152,128]{2,1,0:T(8,128)}), f32[4,152,128]{2,1,0:T(8,128)S(1)}, u32[]{:S(2)}, u32[]{:S(2)}) async-start(f32[4,152,128]{2,1,0:T(8,128)} %broadcast_in_dim.2), calls=%async_computation.1 | async-start | bytes 622592 | tf_op jit(solution)/shard_map/all_to_all | solution.py:172
  27.6 13.0 %collective-permute-start.2 = (f32[152,128]{1,0:T(8,128)S(1)}, f32[152,128]{1,0:T(8,128)S(1)}, u32[]{:S(2)}, u32[]{:S(2)}) collective-permute-start(f32[152,128]{1,0:T(8,128)S(1)} %add.13), channel_id=1, source_target_pairs={{0,8},{2,10},{4,12},{6,14},{8,0},{10,2},{12,4},{14,6},{1,9},{3,11}... | collective-permute-start | bytes 233480 | tf_op jit(solution)/shard_map/ppermute | solution.py:168
  40.7 13.9 %collective-permute-start.3 = (f32[152,128]{1,0:T(8,128)S(1)}, f32[152,128]{1,0:T(8,128)S(1)}, u32[]{:S(2)}, u32[]{:S(2)}) collective-permute-start(f32[152,128]{1,0:T(8,128)S(1)} %add.14), channel_id=1, source_target_pairs={{0,4},{2,6},{4,8},{6,10},{8,12},{10,14},{12,0},{14,2},{1,5},{3,7},... | collective-permute-start | bytes 233480 | tf_op jit(solution)/shard_map/ppermute | solution.py:168
  54.6 5.5 %copy-start.1 = (f32[192,1536]{1,0:T(8,128)S(1)}, f32[192,1536]{1,0:T(8,128)}, u32[]{:S(2)}) copy-start(f32[192,1536]{1,0:T(8,128)} %grad_ref.3) | copy-start | bytes 3538948
  54.6 14.4 %all-to-all-start.2 = ((f32[8,152,128]{2,1,0:T(8,128)}), f32[8,152,128]{2,1,0:T(8,128)S(1)}, u32[]{:S(2)}, u32[]{:S(2)}) async-start(f32[8,152,128]{2,1,0:T(8,128)} %right_root.1), calls=%async_computation.2 | async-start | bytes 1245184 | tf_op jit(solution)/shard_map/all_to_all | solution.py:172

commit v4 on v3

--- a/solution.py
+++ b/solution.py
@@ -187,13 +187,12 @@
         name="grams",
     )(gradient)
     right = swap(right, group)
+    left = left + shift(left, "z", 4)
+    right, left = lax.optimization_barrier((jnp.sum(right, axis=0), left))
+    rest = swap(jnp.broadcast_to(right[None], (lax.axis_size("yh"),) + right.shape), "yh")
     left = left + shift(left, "core", 1)
     left = left + shift(left, "z", 1)
-    right, left = lax.optimization_barrier((jnp.sum(right, axis=0), left))
-    rest = swap(jnp.broadcast_to(right[None], (lax.axis_size("yh"),) + right.shape), "yh")
-    left = left + shift(left, "z", 4)
-    rest, left = lax.optimization_barrier((rest, left))
-    left = left + shift(left, "z", 2)
+    other = shift(left, "z", 2)
 
     roots = pl.pallas_call(
         right_root_kernel,
@@ -203,7 +202,8 @@
         name="right_root",
         cost_estimate=estimate(16 * 10**9),
     )(rest)
-    roots, left = lax.optimization_barrier((roots, left))
+    roots, left, other = lax.optimization_barrier((roots, left, other))
+    left = left + other
     received = swap(roots, group)
 
     high, low = pl.pallas_call(

time: 72.3 us -> 72.6 us (level)
  no operation moved by 1% of the time
where the time goes in v4:
time: 72.6 us; the launch traced here: 72.1 us
  starting transfers between devices  40.2 us (55%)
  Pallas kernels  23 us (32%)
  waiting for transfers between devices  6.83 us (9%)
  local copies, waits for them, and re-layouts  2.01 us (3%)
    ppermute x4, starting transfers between devices, shift(): lax.ppermute(x, axis, [(i, i ^ 1 if by == 1 else (i + by) % n) for i in r...  21.4 us
    all_to_all x3, starting transfers between devices, swap(): return lax.all_to_all(x, axes, 0, 0, tiled=True)  18.8 us
    pallas_call x1, Pallas kernels, body(): pl.pallas_call(right_root_kernel, out_shape=shape(count, PACKED, LANES),...  8.95 us
    pallas_call x1, Pallas kernels, body(): pl.pallas_call(left_root_kernel, out_shape=[shape(count, height, BLOCK, d...  8.84 us
    ppermute x4, waiting for transfers between devices, shift(): lax.ppermute(x, axis, [(i, i ^ 1 if by == 1 else (i + by) % n) for i in r...  6.81 us
    pallas_call x1, Pallas kernels, body(): pl.pallas_call(update_kernel, out_specs=pl.BlockSpec(memory_space=pl.ANY)...  2.82 us
    pallas_call x1, Pallas kernels, body(): pl.pallas_call(gram_kernel, out_shape=[shape(PACKED, LANES), shape(count,...  2.36 us
  transfers between devices with their start and end apart: 7, of which 3 were waited for; matrix products, arithmetic and copies ran while one was open for 0% of the time, Pallas kernels for 25%

profile of v4, /device:TPU:40, one launch (start us, length us, event | category | flops | bytes accessed | tf_op | source)
XLA Modules:
  0.0 72.1 jit_solution(7893584259238091688)
XLA Ops:
  0.0 0.0 copy-start
  0.0 1.3 %copy-done = f32[192,1536]{1,0:T(8,128)S(1)} copy-done((f32[192,1536]{1,0:T(8,128)S(1)}, f32[192,1536]{1,0:T(8,128)}, u32[]{:S(2)}) %copy-start) | copy-done | bytes 1179672
  1.3 2.4 %grams.1 = (f32[152,128]{1,0:T(8,128)S(1)}, f32[8,152,128]{2,1,0:T(8,128)}) custom-call(f32[192,1536]{1,0:T(8,128)S(1)} %copy-done), custom_call_target="tpu_custom_call" | custom-call | tf_op jit(solution)/shard_map/grams/pallas_call | solution.py:183
  3.6 5.8 %all-to-all-start = ((f32[8,152,128]{2,1,0:T(8,128)}), f32[8,152,128]{2,1,0:T(8,128)S(1)}, u32[]{:S(2)}, u32[]{:S(2)}) async-start(f32[8,152,128]{2,1,0:T(8,128)} %get-tuple-element.14), calls=%async_computation | async-start | bytes 1245184 | tf_op jit(solution)/shard_map/all_to_all | solution.py:172
  9.4 10.9 %collective-permute-start = (f32[152,128]{1,0:T(8,128)S(1)}, f32[152,128]{1,0:T(8,128)S(1)}, u32[]{:S(2)}, u32[]{:S(2)}) collective-permute-start(f32[152,128]{1,0:T(8,128)S(1)} %get-tuple-element.15), channel_id=1, source_target_pairs={{0,8},{2,10},{4,12},{6,14},{8,0},{10,2},{12,4},{14,6},{1,9},{3,11}... | collective-permute-start | bytes 233480 | tf_op jit(solution)/shard_map/ppermute | solution.py:168
  20.3 2.9 %collective-permute-done = f32[152,128]{1,0:T(8,128)S(1)} collective-permute-done((f32[152,128]{1,0:T(8,128)S(1)}, f32[152,128]{1,0:T(8,128)S(1)}, u32[]{:S(2)}, u32[]{:S(2)}) %collective-permute-start) | collective-permute-done | bytes 77856 | tf_op jit(solution)/shard_map/ppermute | solution.py:168
  23.2 0.0 all-to-all-done
  23.3 0.7 %broadcast_in_dim.2 = f32[4,152,128]{2,1,0:T(8,128)} broadcast(f32[152,128]{1,0:T(8,128)S(1)} %reduce_sum.9), dimensions={1,2} | broadcast | bytes 389120 | tf_op jit(solution)/shard_map/broadcast_in_dim | solution.py:192
  24.0 7.2 %all-to-all-start.1 = ((f32[4,152,128]{2,1,0:T(8,128)}), f32[4,152,128]{2,1,0:T(8,128)S(1)}, u32[]{:S(2)}, u32[]{:S(2)}) async-start(f32[4,152,128]{2,1,0:T(8,128)} %broadcast_in_dim.2), calls=%async_computation.1 | async-start | bytes 622592 | tf_op jit(solution)/shard_map/all_to_all | solution.py:172
  31.2 1.9 %collective-permute-start.1 = (f32[152,128]{1,0:T(8,128)S(1)}, f32[152,128]{1,0:T(8,128)S(1)}, u32[]{:S(2)}, u32[]{:S(2)}) collective-permute-start(f32[152,128]{1,0:T(8,128)S(1)} %add.12), channel_id=1, source_target_pairs={{0,1},{1,0},{2,3},{3,2},{4,5},{5,4},{6,7},{7,6},{8,9},{9,8},{10,11... | collective-permute-start | bytes 233480 | tf_op jit(solution)/shard_map/ppermute | solution.py:168
  33.1 1.2 %collective-permute-done.1 = f32[152,128]{1,0:T(8,128)S(1)} collective-permute-done((f32[152,128]{1,0:T(8,128)S(1)}, f32[152,128]{1,0:T(8,128)S(1)}, u32[]{:S(2)}, u32[]{:S(2)}) %collective-permute-start.1) | collective-permute-done | bytes 77856 | tf_op jit(solution)/shard_map/ppermute | solution.py:168
  34.4 3.8 %collective-permute-start.2 = (f32[152,128]{1,0:T(8,128)S(1)}, f32[152,128]{1,0:T(8,128)S(1)}, u32[]{:S(2)}, u32[]{:S(2)}) collective-permute-start(f32[152,128]{1,0:T(8,128)S(1)} %add.13), channel_id=1, source_target_pairs={{0,2},{2,0},{4,6},{6,4},{8,10},{10,8},{12,14},{14,12},{1,3},{3,1},... | collective-permute-start | bytes 233480 | tf_op jit(solution)/shard_map/ppermute | solution.py:168
  38.2 2.7 %collective-permute-done.2 = f32[152,128]{1,0:T(8,128)S(1)} collective-permute-done((f32[152,128]{1,0:T(8,128)S(1)}, f32[152,128]{1,0:T(8,128)S(1)}, u32[]{:S(2)}, u32[]{:S(2)}) %collective-permute-start.2) | collective-permute-done | bytes 77856 | tf_op jit(solution)/shard_map/ppermute | solution.py:168
  40.8 4.8 %collective-permute-start.3 = (f32[152,128]{1,0:T(8,128)S(1)}, f32[152,128]{1,0:T(8,128)S(1)}, u32[]{:S(2)}, u32[]{:S(2)}) collective-permute-start(f32[152,128]{1,0:T(8,128)S(1)} %add.14), channel_id=1, source_target_pairs={{0,4},{2,6},{4,8},{6,10},{8,12},{10,14},{12,0},{14,2},{1,5},{3,7},... | collective-permute-start | bytes 233480 | tf_op jit(solution)/shard_map/ppermute | solution.py:168
  45.6 0.0 all-to-all-done.1.parts_ref
  45.6 8.9 %right_root.1 = f32[8,152,128]{2,1,0:T(8,128)} custom-call(f32[4,152,128]{2,1,0:T(8,128)S(1)} %all-to-all-done.1.parts_ref), custom_call_target="tpu_custom_call" | custom-call | flops 16000000000 | bytes 1048576 | tf_op jit(solution)/shard_map/right_root/pallas_call | solution.py:197
  54.6 0.0 copy-start.1
  54.6 0.0 collective-permute-done.3
  54.6 5.8 %all-to-all-start.2 = ((f32[8,152,128]{2,1,0:T(8,128)}), f32[8,152,128]{2,1,0:T(8,128)S(1)}, u32[]{:S(2)}, u32[]{:S(2)}) async-start(f32[8,152,128]{2,1,0:T(8,128)} %right_root.1), calls=%async_computation.2 | async-start | bytes 1245184 | tf_op jit(solution)/shard_map/all_to_all | solution.py:172
  60.5 0.0 copy-done.1
  60.5 8.8 %left_root.1 = (bf16[8,192,192]{2,1,0:T(8,128)(2,1)S(1)}, bf16[8,192,192]{2,1,0:T(8,128)(2,1)S(1)}) custom-call(f32[152,128]{1,0:T(8,128)S(1)} %add.15.gram_ref, f32[192,1536]{1,0:T(8,128)S(1)} %copy-done.1), custom_call_target="tpu_custom_call" | custom-call | flops 8000000000 | bytes 1048576 | tf_op jit(solution)/shard_map/left_root/pallas_call | solution.py:209
  69.3 0.0 all-to-all-done.2.roots_ref
  69.3 2.8 %update.1 = f32[192,1536]{1,0:T(8,128)} custom-call(bf16[8,192,192]{2,1,0:T(8,128)(2,1)S(1)} %get-tuple-element.20.high_ref, bf16[8,192,192]{2,1,0:T(8,128)(2,1)S(1)} %get-tuple-element.21.low_ref, f32[8,152,128]{2,1,0:T(8,128)S(1)} %all-to-all-done.2.roots_ref), custom_call_target="tpu_custom_call" | custom-call | tf_op jit(solution)/shard_map/update/pallas_call | solution.py:217
  (5 shorter events, 0.1 us)
Async XLA Ops:
  0.0 1.3 %copy-start = (f32[192,1536]{1,0:T(8,128)S(1)}, f32[192,1536]{1,0:T(8,128)}, u32[]{:S(2)}) copy-start(f32[192,1536]{1,0:T(8,128)} %grad_ref.3) | copy-start | bytes 3538948
  3.6 19.6 %all-to-all-start = ((f32[8,152,128]{2,1,0:T(8,128)}), f32[8,152,128]{2,1,0:T(8,128)S(1)}, u32[]{:S(2)}, u32[]{:S(2)}) async-start(f32[8,152,128]{2,1,0:T(8,128)} %get-tuple-element.14), calls=%async_computation | async-start | bytes 1245184 | tf_op jit(solution)/shard_map/all_to_all | solution.py:172
  9.4 13.8 %collective-permute-start = (f32[152,128]{1,0:T(8,128)S(1)}, f32[152,128]{1,0:T(8,128)S(1)}, u32[]{:S(2)}, u32[]{:S(2)}) collective-permute-start(f32[152,128]{1,0:T(8,128)S(1)} %get-tuple-element.15), channel_id=1, source_target_pairs={{0,8},{2,10},{4,12},{6,14},{8,0},{10,2},{12,4},{14,6},{1,9},{3,11}... | collective-permute-start | bytes 233480 | tf_op jit(solution)/shard_map/ppermute | solution.py:168
  24.0 21.6 %all-to-all-start.1 = ((f32[4,152,128]{2,1,0:T(8,128)}), f32[4,152,128]{2,1,0:T(8,128)S(1)}, u32[]{:S(2)}, u32[]{:S(2)}) async-start(f32[4,152,128]{2,1,0:T(8,128)} %broadcast_in_dim.2), calls=%async_computation.1 | async-start | bytes 622592 | tf_op jit(solution)/shard_map/all_to_all | solution.py:172
  31.2 3.2 %collective-permute-start.1 = (f32[152,128]{1,0:T(8,128)S(1)}, f32[152,128]{1,0:T(8,128)S(1)}, u32[]{:S(2)}, u32[]{:S(2)}) collective-permute-start(f32[152,128]{1,0:T(8,128)S(1)} %add.12), channel_id=1, source_target_pairs={{0,1},{1,0},{2,3},{3,2},{4,5},{5,4},{6,7},{7,6},{8,9},{9,8},{10,11... | collective-permute-start | bytes 233480 | tf_op jit(solution)/shard_map/ppermute | solution.py:168
  34.4 6.4 %collective-permute-start.2 = (f32[152,128]{1,0:T(8,128)S(1)}, f32[152,128]{1,0:T(8,128)S(1)}, u32[]{:S(2)}, u32[]{:S(2)}) collective-permute-start(f32[152,128]{1,0:T(8,128)S(1)} %add.13), channel_id=1, source_target_pairs={{0,2},{2,0},{4,6},{6,4},{8,10},{10,8},{12,14},{14,12},{1,3},{3,1},... | collective-permute-start | bytes 233480 | tf_op jit(solution)/shard_map/ppermute | solution.py:168
  40.8 13.8 %collective-permute-start.3 = (f32[152,128]{1,0:T(8,128)S(1)}, f32[152,128]{1,0:T(8,128)S(1)}, u32[]{:S(2)}, u32[]{:S(2)}) collective-permute-start(f32[152,128]{1,0:T(8,128)S(1)} %add.14), channel_id=1, source_target_pairs={{0,4},{2,6},{4,8},{6,10},{8,12},{10,14},{12,0},{14,2},{1,5},{3,7},... | collective-permute-start | bytes 233480 | tf_op jit(solution)/shard_map/ppermute | solution.py:168
  54.6 5.9 %copy-start.1 = (f32[192,1536]{1,0:T(8,128)S(1)}, f32[192,1536]{1,0:T(8,128)}, u32[]{:S(2)}) copy-start(f32[192,1536]{1,0:T(8,128)} %grad_ref.3) | copy-start | bytes 3538948
  54.6 14.7 %all-to-all-start.2 = ((f32[8,152,128]{2,1,0:T(8,128)}), f32[8,152,128]{2,1,0:T(8,128)S(1)}, u32[]{:S(2)}, u32[]{:S(2)}) async-start(f32[8,152,128]{2,1,0:T(8,128)} %right_root.1), calls=%async_computation.2 | async-start | bytes 1245184 | tf_op jit(solution)/shard_map/all_to_all | solution.py:172

commit v5 on v4

--- a/solution.py
+++ b/solution.py
@@ -93,16 +93,12 @@
 
     def advance(m):
         parts = split(m)
-        squares = [
-            split(
-                (25.0 * identity[b] - 10.0 * m[b] + product((parts[0][b], parts[1][b]), parts))
-                * 0.0625
-            )
-            for b in bands
+        excess = [
+            split(0.0625 * product((parts[0][b], parts[1][b]), parts) - 0.625 * m[b]) for b in bands
         ]
-        halfway = [split(product(s, parts)) for s in squares]
-        square = [jnp.concatenate([s[k] for s in squares], axis=0) for k in range(2)]
-        return parts, jnp.concatenate([product(h, square) for h in halfway], axis=0)
+        halfway = [1.5625 * m[b] + product(e, parts) for e, b in zip(excess, bands)]
+        whole = [jnp.concatenate([e[k] for e in excess], axis=0) for k in range(2)]
+        return parts, jnp.concatenate([1.5625 * h + product(split(h), whole) for h in halfway], axis=0)
 
     def grow(parts):
         x = x_ref[...]
@@ -119,7 +115,7 @@
         x_ref[...] = grow(parts)
         return carry
 
-    lax.fori_loop(0, ITERS - 2, step, 0, unroll=5)
+    lax.fori_loop(0, ITERS - 2, step, 0, unroll=True)
     return grow(split(m_ref[...])) * lax.rsqrt(jnp.sqrt(norm))
 
 
@@ -140,13 +136,36 @@
             low_ref[2 * k + c] = mid[1][:, window]
 
 
+def halves(p):
+    row, col = grid_of(HALF, HALF)
+    found = []
+    for part in split(p):
+        square = part[:HALF, :HALF]
+        none = jnp.zeros_like(square)
+        middle = part[HALF : HALF + HALF // 2]
+        rest = jnp.concatenate(
+            [part[:HALF, HALF:], jnp.concatenate([middle[:, :64], middle[:, 64:]], axis=0)], axis=1
+        )
+        below = jnp.where(col < row, square, none)
+        diagonal = jnp.broadcast_to(part[144:145, :HALF], (HALF, HALF))
+        for head, tail in (
+            (jnp.where(col >= row, square, none), jnp.where(col == row, diagonal, below)),
+            (jnp.where(col > row, square, none), below),
+        ):
+            top = jnp.concatenate([head, rest], axis=1)
+            found.append(jnp.concatenate([top, jnp.concatenate([none, tail], axis=1)], axis=0))
+    return (found[0], found[2]), (found[1], found[3])
+
+
 def update_kernel(high_ref, low_ref, roots_ref, out_ref, held, sems):
     stores = []
     for k in range(out_ref.shape[1] // CHUNK):
         for c in range(CHUNK // BLOCK):
             b = 2 * k + c
-            root = split(unpack(roots_ref[b]))
-            held[k, :, c * BLOCK : (c + 1) * BLOCK] = product((high_ref[b], low_ref[b]), root) * SCALE
+            mid = (high_ref[b], low_ref[b])
+            plain, flipped = halves(roots_ref[b])
+            block = product(mid, plain) + product(mid, flipped, ((1,), (1,)))
+            held[k, :, c * BLOCK : (c + 1) * BLOCK] = block * SCALE
         stores.append(
             pltpu.make_async_copy(held.at[k], out_ref.at[:, pl.ds(k * CHUNK, CHUNK)], sems.at[k])
         )
@@ -165,7 +184,7 @@
 
 def shift(x, axis, by):
     n = lax.axis_size(axis)
-    return lax.ppermute(x, axis, [(i, i ^ 1 if by == 1 else (i + by) % n) for i in range(n)])
+    return lax.ppermute(x, axis, [(i, (i + by) % n) for i in range(n)])
 
 
 def swap(x, axes):
@@ -191,8 +210,7 @@
     right, left = lax.optimization_barrier((jnp.sum(right, axis=0), left))
     rest = swap(jnp.broadcast_to(right[None], (lax.axis_size("yh"),) + right.shape), "yh")
     left = left + shift(left, "core", 1)
-    left = left + shift(left, "z", 1)
-    other = shift(left, "z", 2)
+    others = [shift(left, "z", by) for by in (1, 7, 2)]
 
     roots = pl.pallas_call(
         right_root_kernel,
@@ -202,8 +220,8 @@
         name="right_root",
         cost_estimate=estimate(16 * 10**9),
     )(rest)
-    roots, left, other = lax.optimization_barrier((roots, left, other))
-    left = left + other
+    roots, left, others = lax.optimization_barrier((roots, left, others))
+    left = sum(others, left)
     received = swap(roots, group)
 
     high, low = pl.pallas_call(

time: 72.6 us -> 73.3 us (level)
  starting transfers between devices: 40.2 us -> 42.8 us
  waiting for transfers between devices: 6.83 us -> 5.03 us
    ppermute x4 -> x5, waiting for transfers between devices: 6.81 us -> 4.15 us  [shift(): return lax.ppermute(x, axis, [(i, (i + by) % n) for i in range(n)])]
    ppermute x4 -> x5, starting transfers between devices: 21.4 us -> 24 us  [shift(): return lax.ppermute(x, axis, [(i, (i + by) % n) for i in range(n)])]
    all_to_all x3, waiting for transfers between devices: 0.01 us -> 0.87 us  [swap(): return lax.all_to_all(x, axes, 0, 0, tiled=True)]
  transfers between devices with their start and end apart: 7 -> 8, of which waited for: 3 -> 3; matrix products, arithmetic and copies ran while one was open for 0% -> 0% of each run, Pallas kernels for 25% -> 24%
where the time goes in v5:
time: 73.3 us; the launch traced here: 72.8 us
  starting transfers between devices  42.8 us (58%)
  Pallas kernels  22.7 us (31%)
  waiting for transfers between devices  5.03 us (7%)
  local copies, waits for them, and re-layouts  2.01 us (3%)
    ppermute x5, starting transfers between devices, shift(): return lax.ppermute(x, axis, [(i, (i + by) % n) for i in range(n)])  24 us
    all_to_all x3, starting transfers between devices, swap(): return lax.all_to_all(x, axes, 0, 0, tiled=True)  18.8 us
    pallas_call x1, Pallas kernels, body(): pl.pallas_call(right_root_kernel, out_shape=shape(count, PACKED, LANES),...  8.9 us
    pallas_call x1, Pallas kernels, body(): pl.pallas_call(left_root_kernel, out_shape=[shape(count, height, BLOCK, d...  8.8 us
    ppermute x5, waiting for transfers between devices, shift(): return lax.ppermute(x, axis, [(i, (i + by) % n) for i in range(n)])  4.15 us
    pallas_call x1, Pallas kernels, body(): pl.pallas_call(update_kernel, out_specs=pl.BlockSpec(memory_space=pl.ANY)...  2.58 us
    pallas_call x1, Pallas kernels, body(): pl.pallas_call(gram_kernel, out_shape=[shape(PACKED, LANES), shape(count,...  2.36 us
  transfers between devices with their start and end apart: 8, of which 3 were waited for; matrix products, arithmetic and copies ran while one was open for 0% of the time, Pallas kernels for 24%

profile of v5, /device:TPU:40, one launch (start us, length us, event | category | flops | bytes accessed | tf_op | source)
XLA Modules:
  0.0 72.8 jit_solution(18188489680112396430)
XLA Ops:
  0.0 0.0 copy-start
  0.0 1.3 %copy-done = f32[192,1536]{1,0:T(8,128)S(1)} copy-done((f32[192,1536]{1,0:T(8,128)S(1)}, f32[192,1536]{1,0:T(8,128)}, u32[]{:S(2)}) %copy-start) | copy-done | bytes 1179672
  1.3 2.4 %grams.1 = (f32[152,128]{1,0:T(8,128)S(1)}, f32[8,152,128]{2,1,0:T(8,128)}) custom-call(f32[192,1536]{1,0:T(8,128)S(1)} %copy-done), custom_call_target="tpu_custom_call" | custom-call | tf_op jit(solution)/shard_map/grams/pallas_call | solution.py:202
  3.6 5.8 %all-to-all-start = ((f32[8,152,128]{2,1,0:T(8,128)}), f32[8,152,128]{2,1,0:T(8,128)S(1)}, u32[]{:S(2)}, u32[]{:S(2)}) async-start(f32[8,152,128]{2,1,0:T(8,128)} %get-tuple-element.16), calls=%async_computation | async-start | bytes 1245184 | tf_op jit(solution)/shard_map/all_to_all | solution.py:191
  9.4 10.9 %collective-permute-start = (f32[152,128]{1,0:T(8,128)S(1)}, f32[152,128]{1,0:T(8,128)S(1)}, u32[]{:S(2)}, u32[]{:S(2)}) collective-permute-start(f32[152,128]{1,0:T(8,128)S(1)} %get-tuple-element.17), channel_id=1, source_target_pairs={{0,8},{2,10},{4,12},{6,14},{8,0},{10,2},{12,4},{14,6},{1,9},{3,11}... | collective-permute-start | bytes 233480 | tf_op jit(solution)/shard_map/ppermute | solution.py:187
  20.3 2.9 %collective-permute-done = f32[152,128]{1,0:T(8,128)S(1)} collective-permute-done((f32[152,128]{1,0:T(8,128)S(1)}, f32[152,128]{1,0:T(8,128)S(1)}, u32[]{:S(2)}, u32[]{:S(2)}) %collective-permute-start) | collective-permute-done | bytes 77856 | tf_op jit(solution)/shard_map/ppermute | solution.py:187
  23.2 0.0 all-to-all-done
  23.3 0.7 %broadcast_in_dim.2 = f32[4,152,128]{2,1,0:T(8,128)} broadcast(f32[152,128]{1,0:T(8,128)S(1)} %reduce_sum.9), dimensions={1,2} | broadcast | bytes 389120 | tf_op jit(solution)/shard_map/broadcast_in_dim | solution.py:211
  24.0 7.2 %all-to-all-start.1 = ((f32[4,152,128]{2,1,0:T(8,128)}), f32[4,152,128]{2,1,0:T(8,128)S(1)}, u32[]{:S(2)}, u32[]{:S(2)}) async-start(f32[4,152,128]{2,1,0:T(8,128)} %broadcast_in_dim.2), calls=%async_computation.1 | async-start | bytes 622592 | tf_op jit(solution)/shard_map/all_to_all | solution.py:191
  31.2 1.9 %collective-permute-start.1 = (f32[152,128]{1,0:T(8,128)S(1)}, f32[152,128]{1,0:T(8,128)S(1)}, u32[]{:S(2)}, u32[]{:S(2)}) collective-permute-start(f32[152,128]{1,0:T(8,128)S(1)} %add.15), channel_id=1, source_target_pairs={{0,1},{1,0},{2,3},{3,2},{4,5},{5,4},{6,7},{7,6},{8,9},{9,8},{10,11... | collective-permute-start | bytes 233480 | tf_op jit(solution)/shard_map/ppermute | solution.py:187
  33.1 1.2 %collective-permute-done.1 = f32[152,128]{1,0:T(8,128)S(1)} collective-permute-done((f32[152,128]{1,0:T(8,128)S(1)}, f32[152,128]{1,0:T(8,128)S(1)}, u32[]{:S(2)}, u32[]{:S(2)}) %collective-permute-start.1) | collective-permute-done | bytes 77856 | tf_op jit(solution)/shard_map/ppermute | solution.py:187
  34.4 4.9 %collective-permute-start.4 = (f32[152,128]{1,0:T(8,128)S(1)}, f32[152,128]{1,0:T(8,128)S(1)}, u32[]{:S(2)}, u32[]{:S(2)}) collective-permute-start(f32[152,128]{1,0:T(8,128)S(1)} %add.16), channel_id=1, source_target_pairs={{0,4},{2,6},{4,8},{6,10},{8,12},{10,14},{12,0},{14,2},{1,5},{3,7},... | collective-permute-start | bytes 233480 | tf_op jit(solution)/shard_map/ppermute | solution.py:187
  39.3 4.3 %collective-permute-start.3 = (f32[152,128]{1,0:T(8,128)S(1)}, f32[152,128]{1,0:T(8,128)S(1)}, u32[]{:S(2)}, u32[]{:S(2)}) collective-permute-start(f32[152,128]{1,0:T(8,128)S(1)} %add.16), channel_id=1, source_target_pairs={{0,14},{2,0},{4,2},{6,4},{8,6},{10,8},{12,10},{14,12},{1,15},{3,1}... | collective-permute-start | bytes 233480 | tf_op jit(solution)/shard_map/ppermute | solution.py:187
  43.6 1.9 %collective-permute-start.2 = (f32[152,128]{1,0:T(8,128)S(1)}, f32[152,128]{1,0:T(8,128)S(1)}, u32[]{:S(2)}, u32[]{:S(2)}) collective-permute-start(f32[152,128]{1,0:T(8,128)S(1)} %add.16), channel_id=1, source_target_pairs={{0,2},{2,4},{4,6},{6,8},{8,10},{10,12},{12,14},{14,0},{1,3},{3,5},... | collective-permute-start | bytes 233480 | tf_op jit(solution)/shard_map/ppermute | solution.py:187
  45.6 0.0 all-to-all-done.1.parts_ref
  45.6 8.9 %right_root.1 = f32[8,152,128]{2,1,0:T(8,128)} custom-call(f32[4,152,128]{2,1,0:T(8,128)S(1)} %all-to-all-done.1.parts_ref), custom_call_target="tpu_custom_call" | custom-call | flops 16000000000 | bytes 1048576 | tf_op jit(solution)/shard_map/right_root/pallas_call | solution.py:215
  54.5 0.0 collective-permute-done.4
  54.5 0.0 collective-permute-done.3
  54.5 0.0 collective-permute-done.2
  54.5 5.8 %all-to-all-start.2 = ((f32[8,152,128]{2,1,0:T(8,128)}), f32[8,152,128]{2,1,0:T(8,128)S(1)}, u32[]{:S(2)}, u32[]{:S(2)}) async-start(f32[8,152,128]{2,1,0:T(8,128)} %right_root.1), calls=%async_computation.2 | async-start | bytes 1245184 | tf_op jit(solution)/shard_map/all_to_all | solution.py:191
  60.4 0.0 copy-done.1
  60.4 8.8 %left_root.1 = (bf16[8,192,192]{2,1,0:T(8,128)(2,1)S(1)}, bf16[8,192,192]{2,1,0:T(8,128)(2,1)S(1)}) custom-call(f32[152,128]{1,0:T(8,128)S(1)} %add_add_fusion.gram_ref, f32[192,1536]{1,0:T(8,128)S(1)} %copy-done.1), custom_call_target="tpu_custom_call" | custom-call | flops 8000000000 | bytes 1048576 | tf_op jit(solution)/shard_map/left_root/pallas_call | solution.py:227
  69.2 0.9 %all-to-all-done.2.roots_ref = f32[8,152,128]{2,1,0:T(8,128)S(1)} async-done(((f32[8,152,128]{2,1,0:T(8,128)}), f32[8,152,128]{2,1,0:T(8,128)S(1)}, u32[]{:S(2)}, u32[]{:S(2)}) %all-to-all-start.2) | async-done | bytes 622624 | tf_op jit(solution)/shard_map/all_to_all | solution.py:191
  70.1 2.6 %update.1 = f32[192,1536]{1,0:T(8,128)} custom-call(bf16[8,192,192]{2,1,0:T(8,128)(2,1)S(1)} %get-tuple-element.24.high_ref, bf16[8,192,192]{2,1,0:T(8,128)(2,1)S(1)} %get-tuple-element.25.low_ref, f32[8,152,128]{2,1,0:T(8,128)S(1)} %all-to-all-done.2.roots_ref), custom_call_target="tpu_custom_call" | custom-call | tf_op jit(solution)/shard_map/update/pallas_call | solution.py:235
  (5 shorter events, 0.1 us)
Async XLA Ops:
  0.0 1.3 %copy-start = (f32[192,1536]{1,0:T(8,128)S(1)}, f32[192,1536]{1,0:T(8,128)}, u32[]{:S(2)}) copy-start(f32[192,1536]{1,0:T(8,128)} %grad_ref.3) | copy-start | bytes 3538948
  3.6 19.6 %all-to-all-start = ((f32[8,152,128]{2,1,0:T(8,128)}), f32[8,152,128]{2,1,0:T(8,128)S(1)}, u32[]{:S(2)}, u32[]{:S(2)}) async-start(f32[8,152,128]{2,1,0:T(8,128)} %get-tuple-element.16), calls=%async_computation | async-start | bytes 1245184 | tf_op jit(solution)/shard_map/all_to_all | solution.py:191
  9.4 13.8 %collective-permute-start = (f32[152,128]{1,0:T(8,128)S(1)}, f32[152,128]{1,0:T(8,128)S(1)}, u32[]{:S(2)}, u32[]{:S(2)}) collective-permute-start(f32[152,128]{1,0:T(8,128)S(1)} %get-tuple-element.17), channel_id=1, source_target_pairs={{0,8},{2,10},{4,12},{6,14},{8,0},{10,2},{12,4},{14,6},{1,9},{3,11}... | collective-permute-start | bytes 233480 | tf_op jit(solution)/shard_map/ppermute | solution.py:187
  24.0 21.5 %all-to-all-start.1 = ((f32[4,152,128]{2,1,0:T(8,128)}), f32[4,152,128]{2,1,0:T(8,128)S(1)}, u32[]{:S(2)}, u32[]{:S(2)}) async-start(f32[4,152,128]{2,1,0:T(8,128)} %broadcast_in_dim.2), calls=%async_computation.1 | async-start | bytes 622592 | tf_op jit(solution)/shard_map/all_to_all | solution.py:191
  31.2 3.2 %collective-permute-start.1 = (f32[152,128]{1,0:T(8,128)S(1)}, f32[152,128]{1,0:T(8,128)S(1)}, u32[]{:S(2)}, u32[]{:S(2)}) collective-permute-start(f32[152,128]{1,0:T(8,128)S(1)} %add.15), channel_id=1, source_target_pairs={{0,1},{1,0},{2,3},{3,2},{4,5},{5,4},{6,7},{7,6},{8,9},{9,8},{10,11... | collective-permute-start | bytes 233480 | tf_op jit(solution)/shard_map/ppermute | solution.py:187
  34.4 20.1 %collective-permute-start.4 = (f32[152,128]{1,0:T(8,128)S(1)}, f32[152,128]{1,0:T(8,128)S(1)}, u32[]{:S(2)}, u32[]{:S(2)}) collective-permute-start(f32[152,128]{1,0:T(8,128)S(1)} %add.16), channel_id=1, source_target_pairs={{0,4},{2,6},{4,8},{6,10},{8,12},{10,14},{12,0},{14,2},{1,5},{3,7},... | collective-permute-start | bytes 233480 | tf_op jit(solution)/shard_map/ppermute | solution.py:187
  39.3 15.2 %collective-permute-start.3 = (f32[152,128]{1,0:T(8,128)S(1)}, f32[152,128]{1,0:T(8,128)S(1)}, u32[]{:S(2)}, u32[]{:S(2)}) collective-permute-start(f32[152,128]{1,0:T(8,128)S(1)} %add.16), channel_id=1, source_target_pairs={{0,14},{2,0},{4,2},{6,4},{8,6},{10,8},{12,10},{14,12},{1,15},{3,1}... | collective-permute-start | bytes 233480 | tf_op jit(solution)/shard_map/ppermute | solution.py:187
  43.6 10.9 %collective-permute-start.2 = (f32[152,128]{1,0:T(8,128)S(1)}, f32[152,128]{1,0:T(8,128)S(1)}, u32[]{:S(2)}, u32[]{:S(2)}) collective-permute-start(f32[152,128]{1,0:T(8,128)S(1)} %add.16), channel_id=1, source_target_pairs={{0,2},{2,4},{4,6},{6,8},{8,10},{10,12},{12,14},{14,0},{1,3},{3,5},... | collective-permute-start | bytes 233480 | tf_op jit(solution)/shard_map/ppermute | solution.py:187
  54.5 5.9 %copy-start.1 = (f32[192,1536]{1,0:T(8,128)S(1)}, f32[192,1536]{1,0:T(8,128)}, u32[]{:S(2)}) copy-start(f32[192,1536]{1,0:T(8,128)} %grad_ref.3) | copy-start | bytes 3538948
  54.5 15.6 %all-to-all-start.2 = ((f32[8,152,128]{2,1,0:T(8,128)}), f32[8,152,128]{2,1,0:T(8,128)S(1)}, u32[]{:S(2)}, u32[]{:S(2)}) async-start(f32[8,152,128]{2,1,0:T(8,128)} %right_root.1), calls=%async_computation.2 | async-start | bytes 1245184 | tf_op jit(solution)/shard_map/all_to_all | solution.py:191

commit v6 on v5

--- a/solution.py
+++ b/solution.py
@@ -187,6 +187,10 @@
     return lax.ppermute(x, axis, [(i, (i + by) % n) for i in range(n)])
 
 
+def other_of_pair(x, axis):
+    return lax.ppermute(x, axis, [(i, i ^ 1) for i in range(lax.axis_size(axis))])
+
+
 def swap(x, axes):
     return lax.all_to_all(x, axes, 0, 0, tiled=True)
 
@@ -206,11 +210,11 @@
         name="grams",
     )(gradient)
     right = swap(right, group)
-    left = left + shift(left, "z", 4)
+    left = left + other_of_pair(left, "core")
+    left = left + other_of_pair(left, "z")
     right, left = lax.optimization_barrier((jnp.sum(right, axis=0), left))
     rest = swap(jnp.broadcast_to(right[None], (lax.axis_size("yh"),) + right.shape), "yh")
-    left = left + shift(left, "core", 1)
-    others = [shift(left, "z", by) for by in (1, 7, 2)]
+    others = [shift(left, "z", by) for by in (2, 6, 4)]
 
     roots = pl.pallas_call(
         right_root_kernel,

time: 73.3 us -> 71.4 us (0.974)
  waiting for transfers between devices: 5.03 us -> 3.91 us
  starting transfers between devices: 42.8 us -> 42 us
    ppermute x5 -> x3, starting transfers between devices: 24 us -> 17.1 us  [shift(): return lax.ppermute(x, axis, [(i, (i + by) % n) for i in range(n)])]
    ppermute x0 -> x2, starting transfers between devices: none -> 6.19 us  [other_of_pair(): lax.ppermute(x, axis, [(i, i ^ 1) for i in range(lax.axis_size(axis))])]
    ppermute x5 -> x3, waiting for transfers between devices: 4.15 us -> 0.01 us  [shift(): return lax.ppermute(x, axis, [(i, (i + by) % n) for i in range(n)])]
    ppermute x0 -> x2, waiting for transfers between devices: none -> 3.9 us  [other_of_pair(): lax.ppermute(x, axis, [(i, i ^ 1) for i in range(lax.axis_size(axis))])]
    all_to_all x3, waiting for transfers between devices: 0.87 us -> 0.01 us  [swap(): return lax.all_to_all(x, axes, 0, 0, tiled=True)]
  transfers between devices with their start and end apart: 8 -> 8, of which waited for: 3 -> 2; matrix products, arithmetic and copies ran while one was open for 0% -> 0% of each run, Pallas kernels for 24% -> 25%
where the time goes in v6:
time: 71.4 us; the launch traced here: 70.9 us
  starting transfers between devices  42 us (59%)
  Pallas kernels  22.7 us (32%)
  waiting for transfers between devices  3.91 us (5%)
  local copies, waits for them, and re-layouts  2.01 us (3%)
    all_to_all x3, starting transfers between devices, swap(): return lax.all_to_all(x, axes, 0, 0, tiled=True)  18.8 us
    ppermute x3, starting transfers between devices, shift(): return lax.ppermute(x, axis, [(i, (i + by) % n) for i in range(n)])  17.1 us
    pallas_call x1, Pallas kernels, body(): pl.pallas_call(right_root_kernel, out_shape=shape(count, PACKED, LANES),...  8.89 us
    pallas_call x1, Pallas kernels, body(): pl.pallas_call(left_root_kernel, out_shape=[shape(count, height, BLOCK, d...  8.8 us
    ppermute x2, starting transfers between devices, other_of_pair(): lax.ppermute(x, axis, [(i, i ^ 1) for i in range(lax.axis_size(axis))])  6.19 us
    ppermute x2, waiting for transfers between devices, other_of_pair(): lax.ppermute(x, axis, [(i, i ^ 1) for i in range(lax.axis_size(axis))])  3.9 us
    pallas_call x1, Pallas kernels, body(): pl.pallas_call(update_kernel, out_specs=pl.BlockSpec(memory_space=pl.ANY)...  2.59 us
    pallas_call x1, Pallas kernels, body(): pl.pallas_call(gram_kernel, out_shape=[shape(PACKED, LANES), shape(count,...  2.36 us
  transfers between devices with their start and end apart: 8, of which 2 were waited for; matrix products, arithmetic and copies ran while one was open for 0% of the time, Pallas kernels for 25%

profile of v6, /device:TPU:40, one launch (start us, length us, event | category | flops | bytes accessed | tf_op | source)
XLA Modules:
  0.0 70.9 jit_solution(12099433119524432361)
XLA Ops:
  0.0 0.0 copy-start
  0.0 1.3 %copy-done = f32[192,1536]{1,0:T(8,128)S(1)} copy-done((f32[192,1536]{1,0:T(8,128)S(1)}, f32[192,1536]{1,0:T(8,128)}, u32[]{:S(2)}) %copy-start) | copy-done | bytes 1179672
  1.3 2.4 %grams.1 = (f32[152,128]{1,0:T(8,128)S(1)}, f32[8,152,128]{2,1,0:T(8,128)}) custom-call(f32[192,1536]{1,0:T(8,128)S(1)} %copy-done), custom_call_target="tpu_custom_call" | custom-call | tf_op jit(solution)/shard_map/grams/pallas_call | solution.py:206
  3.6 5.8 %all-to-all-start = ((f32[8,152,128]{2,1,0:T(8,128)}), f32[8,152,128]{2,1,0:T(8,128)S(1)}, u32[]{:S(2)}, u32[]{:S(2)}) async-start(f32[8,152,128]{2,1,0:T(8,128)} %get-tuple-element.16), calls=%async_computation | async-start | bytes 1245184 | tf_op jit(solution)/shard_map/all_to_all | solution.py:195
  9.4 1.9 %collective-permute-start = (f32[152,128]{1,0:T(8,128)S(1)}, f32[152,128]{1,0:T(8,128)S(1)}, u32[]{:S(2)}, u32[]{:S(2)}) collective-permute-start(f32[152,128]{1,0:T(8,128)S(1)} %get-tuple-element.17), channel_id=1, source_target_pairs={{0,1},{1,0},{2,3},{3,2},{4,5},{5,4},{6,7},{7,6},{8,9},{9,8},{10,11... | collective-permute-start | bytes 233480 | tf_op jit(solution)/shard_map/ppermute | solution.py:191
  11.3 1.2 %collective-permute-done = f32[152,128]{1,0:T(8,128)S(1)} collective-permute-done((f32[152,128]{1,0:T(8,128)S(1)}, f32[152,128]{1,0:T(8,128)S(1)}, u32[]{:S(2)}, u32[]{:S(2)}) %collective-permute-start) | collective-permute-done | bytes 77856 | tf_op jit(solution)/shard_map/ppermute | solution.py:191
  12.6 4.3 %collective-permute-start.1 = (f32[152,128]{1,0:T(8,128)S(1)}, f32[152,128]{1,0:T(8,128)S(1)}, u32[]{:S(2)}, u32[]{:S(2)}) collective-permute-start(f32[152,128]{1,0:T(8,128)S(1)} %add.15), channel_id=1, source_target_pairs={{0,2},{2,0},{4,6},{6,4},{8,10},{10,8},{12,14},{14,12},{1,3},{3,1},... | collective-permute-start | bytes 233480 | tf_op jit(solution)/shard_map/ppermute | solution.py:191
  16.9 2.7 %collective-permute-done.1 = f32[152,128]{1,0:T(8,128)S(1)} collective-permute-done((f32[152,128]{1,0:T(8,128)S(1)}, f32[152,128]{1,0:T(8,128)S(1)}, u32[]{:S(2)}, u32[]{:S(2)}) %collective-permute-start.1) | collective-permute-done | bytes 77856 | tf_op jit(solution)/shard_map/ppermute | solution.py:191
  19.5 0.0 all-to-all-done
  19.6 0.7 %broadcast_in_dim.2 = f32[4,152,128]{2,1,0:T(8,128)} broadcast(f32[152,128]{1,0:T(8,128)S(1)} %reduce_sum.9), dimensions={1,2} | broadcast | bytes 389120 | tf_op jit(solution)/shard_map/broadcast_in_dim | solution.py:216
  20.3 7.3 %all-to-all-start.1 = ((f32[4,152,128]{2,1,0:T(8,128)}), f32[4,152,128]{2,1,0:T(8,128)S(1)}, u32[]{:S(2)}, u32[]{:S(2)}) async-start(f32[4,152,128]{2,1,0:T(8,128)} %broadcast_in_dim.2), calls=%async_computation.1 | async-start | bytes 622592 | tf_op jit(solution)/shard_map/all_to_all | solution.py:195
  27.6 10.3 %collective-permute-start.4 = (f32[152,128]{1,0:T(8,128)S(1)}, f32[152,128]{1,0:T(8,128)S(1)}, u32[]{:S(2)}, u32[]{:S(2)}) collective-permute-start(f32[152,128]{1,0:T(8,128)S(1)} %add.16), channel_id=1, source_target_pairs={{0,8},{2,10},{4,12},{6,14},{8,0},{10,2},{12,4},{14,6},{1,9},{3,11}... | collective-permute-start | bytes 233480 | tf_op jit(solution)/shard_map/ppermute | solution.py:187
  38.0 1.9 %collective-permute-start.3 = (f32[152,128]{1,0:T(8,128)S(1)}, f32[152,128]{1,0:T(8,128)S(1)}, u32[]{:S(2)}, u32[]{:S(2)}) collective-permute-start(f32[152,128]{1,0:T(8,128)S(1)} %add.16), channel_id=1, source_target_pairs={{0,12},{2,14},{4,0},{6,2},{8,4},{10,6},{12,8},{14,10},{1,13},{3,15... | collective-permute-start | bytes 233480 | tf_op jit(solution)/shard_map/ppermute | solution.py:187
  39.9 4.8 %collective-permute-start.2 = (f32[152,128]{1,0:T(8,128)S(1)}, f32[152,128]{1,0:T(8,128)S(1)}, u32[]{:S(2)}, u32[]{:S(2)}) collective-permute-start(f32[152,128]{1,0:T(8,128)S(1)} %add.16), channel_id=1, source_target_pairs={{0,4},{2,6},{4,8},{6,10},{8,12},{10,14},{12,0},{14,2},{1,5},{3,7},... | collective-permute-start | bytes 233480 | tf_op jit(solution)/shard_map/ppermute | solution.py:187
  44.7 0.0 all-to-all-done.1.parts_ref
  44.7 8.9 %right_root.1 = f32[8,152,128]{2,1,0:T(8,128)} custom-call(f32[4,152,128]{2,1,0:T(8,128)S(1)} %all-to-all-done.1.parts_ref), custom_call_target="tpu_custom_call" | custom-call | flops 16000000000 | bytes 1048576 | tf_op jit(solution)/shard_map/right_root/pallas_call | solution.py:219
  53.6 0.0 collective-permute-done.4
  53.6 0.0 collective-permute-done.3
  53.6 0.0 collective-permute-done.2
  53.6 5.7 %all-to-all-start.2 = ((f32[8,152,128]{2,1,0:T(8,128)}), f32[8,152,128]{2,1,0:T(8,128)S(1)}, u32[]{:S(2)}, u32[]{:S(2)}) async-start(f32[8,152,128]{2,1,0:T(8,128)} %right_root.1), calls=%async_computation.2 | async-start | bytes 1245184 | tf_op jit(solution)/shard_map/all_to_all | solution.py:195
  59.4 0.0 copy-done.1
  59.4 8.8 %left_root.1 = (bf16[8,192,192]{2,1,0:T(8,128)(2,1)S(1)}, bf16[8,192,192]{2,1,0:T(8,128)(2,1)S(1)}) custom-call(f32[152,128]{1,0:T(8,128)S(1)} %add_add_fusion.gram_ref, f32[192,1536]{1,0:T(8,128)S(1)} %copy-done.1), custom_call_target="tpu_custom_call" | custom-call | flops 8000000000 | bytes 1048576 | tf_op jit(solution)/shard_map/left_root/pallas_call | solution.py:231
  68.2 0.0 all-to-all-done.2.roots_ref
  68.2 2.6 %update.1 = f32[192,1536]{1,0:T(8,128)} custom-call(bf16[8,192,192]{2,1,0:T(8,128)(2,1)S(1)} %get-tuple-element.24.high_ref, bf16[8,192,192]{2,1,0:T(8,128)(2,1)S(1)} %get-tuple-element.25.low_ref, f32[8,152,128]{2,1,0:T(8,128)S(1)} %all-to-all-done.2.roots_ref), custom_call_target="tpu_custom_call" | custom-call | tf_op jit(solution)/shard_map/update/pallas_call | solution.py:239
  (5 shorter events, 0.1 us)
Async XLA Ops:
  0.0 1.3 %copy-start = (f32[192,1536]{1,0:T(8,128)S(1)}, f32[192,1536]{1,0:T(8,128)}, u32[]{:S(2)}) copy-start(f32[192,1536]{1,0:T(8,128)} %grad_ref.3) | copy-start | bytes 3538948
  3.6 15.9 %all-to-all-start = ((f32[8,152,128]{2,1,0:T(8,128)}), f32[8,152,128]{2,1,0:T(8,128)S(1)}, u32[]{:S(2)}, u32[]{:S(2)}) async-start(f32[8,152,128]{2,1,0:T(8,128)} %get-tuple-element.16), calls=%async_computation | async-start | bytes 1245184 | tf_op jit(solution)/shard_map/all_to_all | solution.py:195
  9.4 3.2 %collective-permute-start = (f32[152,128]{1,0:T(8,128)S(1)}, f32[152,128]{1,0:T(8,128)S(1)}, u32[]{:S(2)}, u32[]{:S(2)}) collective-permute-start(f32[152,128]{1,0:T(8,128)S(1)} %get-tuple-element.17), channel_id=1, source_target_pairs={{0,1},{1,0},{2,3},{3,2},{4,5},{5,4},{6,7},{7,6},{8,9},{9,8},{10,11... | collective-permute-start | bytes 233480 | tf_op jit(solution)/shard_map/ppermute | solution.py:191
  12.6 7.0 %collective-permute-start.1 = (f32[152,128]{1,0:T(8,128)S(1)}, f32[152,128]{1,0:T(8,128)S(1)}, u32[]{:S(2)}, u32[]{:S(2)}) collective-permute-start(f32[152,128]{1,0:T(8,128)S(1)} %add.15), channel_id=1, source_target_pairs={{0,2},{2,0},{4,6},{6,4},{8,10},{10,8},{12,14},{14,12},{1,3},{3,1},... | collective-permute-start | bytes 233480 | tf_op jit(solution)/shard_map/ppermute | solution.py:191
  20.3 24.4 %all-to-all-start.1 = ((f32[4,152,128]{2,1,0:T(8,128)}), f32[4,152,128]{2,1,0:T(8,128)S(1)}, u32[]{:S(2)}, u32[]{:S(2)}) async-start(f32[4,152,128]{2,1,0:T(8,128)} %broadcast_in_dim.2), calls=%async_computation.1 | async-start | bytes 622592 | tf_op jit(solution)/shard_map/all_to_all | solution.py:195
  27.6 26.0 %collective-permute-start.4 = (f32[152,128]{1,0:T(8,128)S(1)}, f32[152,128]{1,0:T(8,128)S(1)}, u32[]{:S(2)}, u32[]{:S(2)}) collective-permute-start(f32[152,128]{1,0:T(8,128)S(1)} %add.16), channel_id=1, source_target_pairs={{0,8},{2,10},{4,12},{6,14},{8,0},{10,2},{12,4},{14,6},{1,9},{3,11}... | collective-permute-start | bytes 233480 | tf_op jit(solution)/shard_map/ppermute | solution.py:187
  38.0 15.7 %collective-permute-start.3 = (f32[152,128]{1,0:T(8,128)S(1)}, f32[152,128]{1,0:T(8,128)S(1)}, u32[]{:S(2)}, u32[]{:S(2)}) collective-permute-start(f32[152,128]{1,0:T(8,128)S(1)} %add.16), channel_id=1, source_target_pairs={{0,12},{2,14},{4,0},{6,2},{8,4},{10,6},{12,8},{14,10},{1,13},{3,15... | collective-permute-start | bytes 233480 | tf_op jit(solution)/shard_map/ppermute | solution.py:187
  39.9 13.7 %collective-permute-start.2 = (f32[152,128]{1,0:T(8,128)S(1)}, f32[152,128]{1,0:T(8,128)S(1)}, u32[]{:S(2)}, u32[]{:S(2)}) collective-permute-start(f32[152,128]{1,0:T(8,128)S(1)} %add.16), channel_id=1, source_target_pairs={{0,4},{2,6},{4,8},{6,10},{8,12},{10,14},{12,0},{14,2},{1,5},{3,7},... | collective-permute-start | bytes 233480 | tf_op jit(solution)/shard_map/ppermute | solution.py:187
  53.6 5.7 %copy-start.1 = (f32[192,1536]{1,0:T(8,128)S(1)}, f32[192,1536]{1,0:T(8,128)}, u32[]{:S(2)}) copy-start(f32[192,1536]{1,0:T(8,128)} %grad_ref.3) | copy-start | bytes 3538948
  53.6 14.5 %all-to-all-start.2 = ((f32[8,152,128]{2,1,0:T(8,128)}), f32[8,152,128]{2,1,0:T(8,128)S(1)}, u32[]{:S(2)}, u32[]{:S(2)}) async-start(f32[8,152,128]{2,1,0:T(8,128)} %right_root.1), calls=%async_computation.2 | async-start | bytes 1245184 | tf_op jit(solution)/shard_map/all_to_all | solution.py:195

commit v7 on v6

--- a/solution.py
+++ b/solution.py
@@ -214,7 +214,7 @@
     left = left + other_of_pair(left, "z")
     right, left = lax.optimization_barrier((jnp.sum(right, axis=0), left))
     rest = swap(jnp.broadcast_to(right[None], (lax.axis_size("yh"),) + right.shape), "yh")
-    others = [shift(left, "z", by) for by in (2, 6, 4)]
+    others = [shift(left, "z", by) for by in (4, 6, 2)]
 
     roots = pl.pallas_call(
         right_root_kernel,

time: 71.4 us -> 72.7 us (1.018)
  starting transfers between devices: 42 us -> 43.2 us
    ppermute x3, starting transfers between devices: 17.1 us -> 18.3 us  [shift(): return lax.ppermute(x, axis, [(i, (i + by) % n) for i in range(n)])]
where the time goes in v7:
time: 72.7 us; the launch traced here: 72.2 us
  starting transfers between devices  43.2 us (59%)
  Pallas kernels  22.7 us (31%)
  waiting for transfers between devices  3.91 us (5%)
  local copies, waits for them, and re-layouts  2.01 us (3%)
    all_to_all x3, starting transfers between devices, swap(): return lax.all_to_all(x, axes, 0, 0, tiled=True)  18.8 us
    ppermute x3, starting transfers between devices, shift(): return lax.ppermute(x, axis, [(i, (i + by) % n) for i in range(n)])  18.3 us
    pallas_call x1, Pallas kernels, body(): pl.pallas_call(right_root_kernel, out_shape=shape(count, PACKED, LANES),...  8.9 us
    pallas_call x1, Pallas kernels, body(): pl.pallas_call(left_root_kernel, out_shape=[shape(count, height, BLOCK, d...  8.8 us
    ppermute x2, starting transfers between devices, other_of_pair(): lax.ppermute(x, axis, [(i, i ^ 1) for i in range(lax.axis_size(axis))])  6.19 us
    ppermute x2, waiting for transfers between devices, other_of_pair(): lax.ppermute(x, axis, [(i, i ^ 1) for i in range(lax.axis_size(axis))])  3.9 us
    pallas_call x1, Pallas kernels, body(): pl.pallas_call(update_kernel, out_specs=pl.BlockSpec(memory_space=pl.ANY)...  2.59 us
    pallas_call x1, Pallas kernels, body(): pl.pallas_call(gram_kernel, out_shape=[shape(PACKED, LANES), shape(count,...  2.36 us
  transfers between devices with their start and end apart: 8, of which 2 were waited for; matrix products, arithmetic and copies ran while one was open for 0% of the time, Pallas kernels for 25%

profile of v7, /device:TPU:40, one launch (start us, length us, event | category | flops | bytes accessed | tf_op | source)
XLA Modules:
  0.0 72.2 jit_solution(4946240212245806586)
XLA Ops:
  0.0 0.0 copy-start
  0.0 1.3 %copy-done = f32[192,1536]{1,0:T(8,128)S(1)} copy-done((f32[192,1536]{1,0:T(8,128)S(1)}, f32[192,1536]{1,0:T(8,128)}, u32[]{:S(2)}) %copy-start) | copy-done | bytes 1179672
  1.3 2.4 %grams.1 = (f32[152,128]{1,0:T(8,128)S(1)}, f32[8,152,128]{2,1,0:T(8,128)}) custom-call(f32[192,1536]{1,0:T(8,128)S(1)} %copy-done), custom_call_target="tpu_custom_call" | custom-call | tf_op jit(solution)/shard_map/grams/pallas_call | solution.py:206
  3.6 5.8 %all-to-all-start = ((f32[8,152,128]{2,1,0:T(8,128)}), f32[8,152,128]{2,1,0:T(8,128)S(1)}, u32[]{:S(2)}, u32[]{:S(2)}) async-start(f32[8,152,128]{2,1,0:T(8,128)} %get-tuple-element.16), calls=%async_computation | async-start | bytes 1245184 | tf_op jit(solution)/shard_map/all_to_all | solution.py:195
  9.4 1.9 %collective-permute-start = (f32[152,128]{1,0:T(8,128)S(1)}, f32[152,128]{1,0:T(8,128)S(1)}, u32[]{:S(2)}, u32[]{:S(2)}) collective-permute-start(f32[152,128]{1,0:T(8,128)S(1)} %get-tuple-element.17), channel_id=1, source_target_pairs={{0,1},{1,0},{2,3},{3,2},{4,5},{5,4},{6,7},{7,6},{8,9},{9,8},{10,11... | collective-permute-start | bytes 233480 | tf_op jit(solution)/shard_map/ppermute | solution.py:191
  11.3 1.2 %collective-permute-done = f32[152,128]{1,0:T(8,128)S(1)} collective-permute-done((f32[152,128]{1,0:T(8,128)S(1)}, f32[152,128]{1,0:T(8,128)S(1)}, u32[]{:S(2)}, u32[]{:S(2)}) %collective-permute-start) | collective-permute-done | bytes 77856 | tf_op jit(solution)/shard_map/ppermute | solution.py:191
  12.6 4.3 %collective-permute-start.1 = (f32[152,128]{1,0:T(8,128)S(1)}, f32[152,128]{1,0:T(8,128)S(1)}, u32[]{:S(2)}, u32[]{:S(2)}) collective-permute-start(f32[152,128]{1,0:T(8,128)S(1)} %add.15), channel_id=1, source_target_pairs={{0,2},{2,0},{4,6},{6,4},{8,10},{10,8},{12,14},{14,12},{1,3},{3,1},... | collective-permute-start | bytes 233480 | tf_op jit(solution)/shard_map/ppermute | solution.py:191
  16.9 2.7 %collective-permute-done.1 = f32[152,128]{1,0:T(8,128)S(1)} collective-permute-done((f32[152,128]{1,0:T(8,128)S(1)}, f32[152,128]{1,0:T(8,128)S(1)}, u32[]{:S(2)}, u32[]{:S(2)}) %collective-permute-start.1) | collective-permute-done | bytes 77856 | tf_op jit(solution)/shard_map/ppermute | solution.py:191
  19.5 0.0 all-to-all-done
  19.6 0.7 %broadcast_in_dim.2 = f32[4,152,128]{2,1,0:T(8,128)} broadcast(f32[152,128]{1,0:T(8,128)S(1)} %reduce_sum.9), dimensions={1,2} | broadcast | bytes 389120 | tf_op jit(solution)/shard_map/broadcast_in_dim | solution.py:216
  20.3 7.3 %all-to-all-start.1 = ((f32[4,152,128]{2,1,0:T(8,128)}), f32[4,152,128]{2,1,0:T(8,128)S(1)}, u32[]{:S(2)}, u32[]{:S(2)}) async-start(f32[4,152,128]{2,1,0:T(8,128)} %broadcast_in_dim.2), calls=%async_computation.1 | async-start | bytes 622592 | tf_op jit(solution)/shard_map/all_to_all | solution.py:195
  27.6 6.0 %collective-permute-start.4 = (f32[152,128]{1,0:T(8,128)S(1)}, f32[152,128]{1,0:T(8,128)S(1)}, u32[]{:S(2)}, u32[]{:S(2)}) collective-permute-start(f32[152,128]{1,0:T(8,128)S(1)} %add.16), channel_id=1, source_target_pairs={{0,4},{2,6},{4,8},{6,10},{8,12},{10,14},{12,0},{14,2},{1,5},{3,7},... | collective-permute-start | bytes 233480 | tf_op jit(solution)/shard_map/ppermute | solution.py:187
  33.6 6.3 %collective-permute-start.3 = (f32[152,128]{1,0:T(8,128)S(1)}, f32[152,128]{1,0:T(8,128)S(1)}, u32[]{:S(2)}, u32[]{:S(2)}) collective-permute-start(f32[152,128]{1,0:T(8,128)S(1)} %add.16), channel_id=1, source_target_pairs={{0,12},{2,14},{4,0},{6,2},{8,4},{10,6},{12,8},{14,10},{1,13},{3,15... | collective-permute-start | bytes 233480 | tf_op jit(solution)/shard_map/ppermute | solution.py:187
  39.9 6.0 %collective-permute-start.2 = (f32[152,128]{1,0:T(8,128)S(1)}, f32[152,128]{1,0:T(8,128)S(1)}, u32[]{:S(2)}, u32[]{:S(2)}) collective-permute-start(f32[152,128]{1,0:T(8,128)S(1)} %add.16), channel_id=1, source_target_pairs={{0,8},{2,10},{4,12},{6,14},{8,0},{10,2},{12,4},{14,6},{1,9},{3,11}... | collective-permute-start | bytes 233480 | tf_op jit(solution)/shard_map/ppermute | solution.py:187
  45.9 0.0 all-to-all-done.1.parts_ref
  45.9 8.9 %right_root.1 = f32[8,152,128]{2,1,0:T(8,128)} custom-call(f32[4,152,128]{2,1,0:T(8,128)S(1)} %all-to-all-done.1.parts_ref), custom_call_target="tpu_custom_call" | custom-call | flops 16000000000 | bytes 1048576 | tf_op jit(solution)/shard_map/right_root/pallas_call | solution.py:219
  54.8 0.0 collective-permute-done.4
  54.8 0.0 collective-permute-done.3
  54.8 0.0 collective-permute-done.2
  54.9 5.7 %all-to-all-start.2 = ((f32[8,152,128]{2,1,0:T(8,128)}), f32[8,152,128]{2,1,0:T(8,128)S(1)}, u32[]{:S(2)}, u32[]{:S(2)}) async-start(f32[8,152,128]{2,1,0:T(8,128)} %right_root.1), calls=%async_computation.2 | async-start | bytes 1245184 | tf_op jit(solution)/shard_map/all_to_all | solution.py:195
  60.6 0.0 copy-done.1
  60.6 8.8 %left_root.1 = (bf16[8,192,192]{2,1,0:T(8,128)(2,1)S(1)}, bf16[8,192,192]{2,1,0:T(8,128)(2,1)S(1)}) custom-call(f32[152,128]{1,0:T(8,128)S(1)} %add_add_fusion.gram_ref, f32[192,1536]{1,0:T(8,128)S(1)} %copy-done.1), custom_call_target="tpu_custom_call" | custom-call | flops 8000000000 | bytes 1048576 | tf_op jit(solution)/shard_map/left_root/pallas_call | solution.py:231
  69.4 0.0 all-to-all-done.2.roots_ref
  69.4 2.6 %update.1 = f32[192,1536]{1,0:T(8,128)} custom-call(bf16[8,192,192]{2,1,0:T(8,128)(2,1)S(1)} %get-tuple-element.24.high_ref, bf16[8,192,192]{2,1,0:T(8,128)(2,1)S(1)} %get-tuple-element.25.low_ref, f32[8,152,128]{2,1,0:T(8,128)S(1)} %all-to-all-done.2.roots_ref), custom_call_target="tpu_custom_call" | custom-call | tf_op jit(solution)/shard_map/update/pallas_call | solution.py:239
  (5 shorter events, 0.1 us)
Async XLA Ops:
  0.0 1.3 %copy-start = (f32[192,1536]{1,0:T(8,128)S(1)}, f32[192,1536]{1,0:T(8,128)}, u32[]{:S(2)}) copy-start(f32[192,1536]{1,0:T(8,128)} %grad_ref.3) | copy-start | bytes 3538948
  3.6 15.9 %all-to-all-start = ((f32[8,152,128]{2,1,0:T(8,128)}), f32[8,152,128]{2,1,0:T(8,128)S(1)}, u32[]{:S(2)}, u32[]{:S(2)}) async-start(f32[8,152,128]{2,1,0:T(8,128)} %get-tuple-element.16), calls=%async_computation | async-start | bytes 1245184 | tf_op jit(solution)/shard_map/all_to_all | solution.py:195
  9.4 3.2 %collective-permute-start = (f32[152,128]{1,0:T(8,128)S(1)}, f32[152,128]{1,0:T(8,128)S(1)}, u32[]{:S(2)}, u32[]{:S(2)}) collective-permute-start(f32[152,128]{1,0:T(8,128)S(1)} %get-tuple-element.17), channel_id=1, source_target_pairs={{0,1},{1,0},{2,3},{3,2},{4,5},{5,4},{6,7},{7,6},{8,9},{9,8},{10,11... | collective-permute-start | bytes 233480 | tf_op jit(solution)/shard_map/ppermute | solution.py:191
  12.6 7.0 %collective-permute-start.1 = (f32[152,128]{1,0:T(8,128)S(1)}, f32[152,128]{1,0:T(8,128)S(1)}, u32[]{:S(2)}, u32[]{:S(2)}) collective-permute-start(f32[152,128]{1,0:T(8,128)S(1)} %add.15), channel_id=1, source_target_pairs={{0,2},{2,0},{4,6},{6,4},{8,10},{10,8},{12,14},{14,12},{1,3},{3,1},... | collective-permute-start | bytes 233480 | tf_op jit(solution)/shard_map/ppermute | solution.py:191
  20.3 25.6 %all-to-all-start.1 = ((f32[4,152,128]{2,1,0:T(8,128)}), f32[4,152,128]{2,1,0:T(8,128)S(1)}, u32[]{:S(2)}, u32[]{:S(2)}) async-start(f32[4,152,128]{2,1,0:T(8,128)} %broadcast_in_dim.2), calls=%async_computation.1 | async-start | bytes 622592 | tf_op jit(solution)/shard_map/all_to_all | solution.py:195
  27.6 27.2 %collective-permute-start.4 = (f32[152,128]{1,0:T(8,128)S(1)}, f32[152,128]{1,0:T(8,128)S(1)}, u32[]{:S(2)}, u32[]{:S(2)}) collective-permute-start(f32[152,128]{1,0:T(8,128)S(1)} %add.16), channel_id=1, source_target_pairs={{0,4},{2,6},{4,8},{6,10},{8,12},{10,14},{12,0},{14,2},{1,5},{3,7},... | collective-permute-start | bytes 233480 | tf_op jit(solution)/shard_map/ppermute | solution.py:187
  33.6 21.2 %collective-permute-start.3 = (f32[152,128]{1,0:T(8,128)S(1)}, f32[152,128]{1,0:T(8,128)S(1)}, u32[]{:S(2)}, u32[]{:S(2)}) collective-permute-start(f32[152,128]{1,0:T(8,128)S(1)} %add.16), channel_id=1, source_target_pairs={{0,12},{2,14},{4,0},{6,2},{8,4},{10,6},{12,8},{14,10},{1,13},{3,15... | collective-permute-start | bytes 233480 | tf_op jit(solution)/shard_map/ppermute | solution.py:187
  39.9 14.9 %collective-permute-start.2 = (f32[152,128]{1,0:T(8,128)S(1)}, f32[152,128]{1,0:T(8,128)S(1)}, u32[]{:S(2)}, u32[]{:S(2)}) collective-permute-start(f32[152,128]{1,0:T(8,128)S(1)} %add.16), channel_id=1, source_target_pairs={{0,8},{2,10},{4,12},{6,14},{8,0},{10,2},{12,4},{14,6},{1,9},{3,11}... | collective-permute-start | bytes 233480 | tf_op jit(solution)/shard_map/ppermute | solution.py:187
  54.8 5.7 %copy-start.1 = (f32[192,1536]{1,0:T(8,128)S(1)}, f32[192,1536]{1,0:T(8,128)}, u32[]{:S(2)}) copy-start(f32[192,1536]{1,0:T(8,128)} %grad_ref.3) | copy-start | bytes 3538948
  54.9 14.5 %all-to-all-start.2 = ((f32[8,152,128]{2,1,0:T(8,128)}), f32[8,152,128]{2,1,0:T(8,128)S(1)}, u32[]{:S(2)}, u32[]{:S(2)}) async-start(f32[8,152,128]{2,1,0:T(8,128)} %right_root.1), calls=%async_computation.2 | async-start | bytes 1245184 | tf_op jit(solution)/shard_map/all_to_all | solution.py:195

commit v8 on v5

--- a/solution.py
+++ b/solution.py
@@ -182,9 +182,8 @@
     return pl.CostEstimate(flops=flops, bytes_accessed=2**20, transcendentals=0)
 
 
-def shift(x, axis, by):
-    n = lax.axis_size(axis)
-    return lax.ppermute(x, axis, [(i, (i + by) % n) for i in range(n)])
+def partner(x, axis, bits):
+    return lax.ppermute(x, axis, [(i, i ^ bits) for i in range(lax.axis_size(axis))])
 
 
 def swap(x, axes):
@@ -206,11 +205,11 @@
         name="grams",
     )(gradient)
     right = swap(right, group)
-    left = left + shift(left, "z", 4)
+    left = left + partner(left, "core", 1)
+    left = left + partner(left, "z", 1)
     right, left = lax.optimization_barrier((jnp.sum(right, axis=0), left))
     rest = swap(jnp.broadcast_to(right[None], (lax.axis_size("yh"),) + right.shape), "yh")
-    left = left + shift(left, "core", 1)
-    others = [shift(left, "z", by) for by in (1, 7, 2)]
+    others = [partner(left, "z", bits) for bits in (2, 6, 4)]
 
     roots = pl.pallas_call(
         right_root_kernel,

time: 73.3 us -> 70.9 us (0.967)
  starting transfers between devices: 42.8 us -> 41.5 us
  waiting for transfers between devices: 5.03 us -> 3.91 us
    ppermute x5, starting transfers between devices: 24 us -> 22.7 us  [partner(): lax.ppermute(x, axis, [(i, i ^ bits) for i in range(lax.axis_size(axis))])]
    all_to_all x3, waiting for transfers between devices: 0.87 us -> 0.01 us  [swap(): return lax.all_to_all(x, axes, 0, 0, tiled=True)]
  transfers between devices with their start and end apart: 8 -> 8, of which waited for: 3 -> 2; matrix products, arithmetic and copies ran while one was open for 0% -> 0% of each run, Pallas kernels for 24% -> 25%
where the time goes in v8:
time: 70.9 us; the launch traced here: 70.4 us
  starting transfers between devices  41.5 us (59%)
  Pallas kernels  22.7 us (32%)
  waiting for transfers between devices  3.91 us (6%)
  local copies, waits for them, and re-layouts  2.01 us (3%)
    ppermute x5, starting transfers between devices, partner(): lax.ppermute(x, axis, [(i, i ^ bits) for i in range(lax.axis_size(axis))])  22.7 us
    all_to_all x3, starting transfers between devices, swap(): return lax.all_to_all(x, axes, 0, 0, tiled=True)  18.8 us
    pallas_call x1, Pallas kernels, body(): pl.pallas_call(right_root_kernel, out_shape=shape(count, PACKED, LANES),...  8.9 us
    pallas_call x1, Pallas kernels, body(): pl.pallas_call(left_root_kernel, out_shape=[shape(count, height, BLOCK, d...  8.8 us
    ppermute x5, waiting for transfers between devices, partner(): lax.ppermute(x, axis, [(i, i ^ bits) for i in range(lax.axis_size(axis))])  3.91 us
    pallas_call x1, Pallas kernels, body(): pl.pallas_call(update_kernel, out_specs=pl.BlockSpec(memory_space=pl.ANY)...  2.59 us
    pallas_call x1, Pallas kernels, body(): pl.pallas_call(gram_kernel, out_shape=[shape(PACKED, LANES), shape(count,...  2.36 us
  transfers between devices with their start and end apart: 8, of which 2 were waited for; matrix products, arithmetic and copies ran while one was open for 0% of the time, Pallas kernels for 25%

profile of v8, /device:TPU:40, one launch (start us, length us, event | category | flops | bytes accessed | tf_op | source)
XLA Modules:
  0.0 70.4 jit_solution(12547905714585405168)
XLA Ops:
  0.0 0.0 copy-start
  0.0 1.3 %copy-done = f32[192,1536]{1,0:T(8,128)S(1)} copy-done((f32[192,1536]{1,0:T(8,128)S(1)}, f32[192,1536]{1,0:T(8,128)}, u32[]{:S(2)}) %copy-start) | copy-done | bytes 1179672
  1.3 2.4 %grams.1 = (f32[152,128]{1,0:T(8,128)S(1)}, f32[8,152,128]{2,1,0:T(8,128)}) custom-call(f32[192,1536]{1,0:T(8,128)S(1)} %copy-done), custom_call_target="tpu_custom_call" | custom-call | tf_op jit(solution)/shard_map/grams/pallas_call | solution.py:201
  3.6 5.8 %all-to-all-start = ((f32[8,152,128]{2,1,0:T(8,128)}), f32[8,152,128]{2,1,0:T(8,128)S(1)}, u32[]{:S(2)}, u32[]{:S(2)}) async-start(f32[8,152,128]{2,1,0:T(8,128)} %get-tuple-element.16), calls=%async_computation | async-start | bytes 1245184 | tf_op jit(solution)/shard_map/all_to_all | solution.py:190
  9.4 1.9 %collective-permute-start = (f32[152,128]{1,0:T(8,128)S(1)}, f32[152,128]{1,0:T(8,128)S(1)}, u32[]{:S(2)}, u32[]{:S(2)}) collective-permute-start(f32[152,128]{1,0:T(8,128)S(1)} %get-tuple-element.17), channel_id=1, source_target_pairs={{0,1},{1,0},{2,3},{3,2},{4,5},{5,4},{6,7},{7,6},{8,9},{9,8},{10,11... | collective-permute-start | bytes 233480 | tf_op jit(solution)/shard_map/ppermute | solution.py:186
  11.3 1.2 %collective-permute-done = f32[152,128]{1,0:T(8,128)S(1)} collective-permute-done((f32[152,128]{1,0:T(8,128)S(1)}, f32[152,128]{1,0:T(8,128)S(1)}, u32[]{:S(2)}, u32[]{:S(2)}) %collective-permute-start) | collective-permute-done | bytes 77856 | tf_op jit(solution)/shard_map/ppermute | solution.py:186
  12.6 4.3 %collective-permute-start.1 = (f32[152,128]{1,0:T(8,128)S(1)}, f32[152,128]{1,0:T(8,128)S(1)}, u32[]{:S(2)}, u32[]{:S(2)}) collective-permute-start(f32[152,128]{1,0:T(8,128)S(1)} %add.15), channel_id=1, source_target_pairs={{0,2},{2,0},{4,6},{6,4},{8,10},{10,8},{12,14},{14,12},{1,3},{3,1},... | collective-permute-start | bytes 233480 | tf_op jit(solution)/shard_map/ppermute | solution.py:186
  16.9 2.7 %collective-permute-done.1 = f32[152,128]{1,0:T(8,128)S(1)} collective-permute-done((f32[152,128]{1,0:T(8,128)S(1)}, f32[152,128]{1,0:T(8,128)S(1)}, u32[]{:S(2)}, u32[]{:S(2)}) %collective-permute-start.1) | collective-permute-done | bytes 77856 | tf_op jit(solution)/shard_map/ppermute | solution.py:186
  19.5 0.0 all-to-all-done
  19.6 0.7 %broadcast_in_dim.2 = f32[4,152,128]{2,1,0:T(8,128)} broadcast(f32[152,128]{1,0:T(8,128)S(1)} %reduce_sum.9), dimensions={1,2} | broadcast | bytes 389120 | tf_op jit(solution)/shard_map/broadcast_in_dim | solution.py:211
  20.3 7.3 %all-to-all-start.1 = ((f32[4,152,128]{2,1,0:T(8,128)}), f32[4,152,128]{2,1,0:T(8,128)S(1)}, u32[]{:S(2)}, u32[]{:S(2)}) async-start(f32[4,152,128]{2,1,0:T(8,128)} %broadcast_in_dim.2), calls=%async_computation.1 | async-start | bytes 622592 | tf_op jit(solution)/shard_map/all_to_all | solution.py:190
  27.6 10.3 %collective-permute-start.4 = (f32[152,128]{1,0:T(8,128)S(1)}, f32[152,128]{1,0:T(8,128)S(1)}, u32[]{:S(2)}, u32[]{:S(2)}) collective-permute-start(f32[152,128]{1,0:T(8,128)S(1)} %add.16), channel_id=1, source_target_pairs={{0,8},{2,10},{4,12},{6,14},{8,0},{10,2},{12,4},{14,6},{1,9},{3,11}... | collective-permute-start | bytes 233480 | tf_op jit(solution)/shard_map/ppermute | solution.py:186
  38.0 1.9 %collective-permute-start.3 = (f32[152,128]{1,0:T(8,128)S(1)}, f32[152,128]{1,0:T(8,128)S(1)}, u32[]{:S(2)}, u32[]{:S(2)}) collective-permute-start(f32[152,128]{1,0:T(8,128)S(1)} %add.16), channel_id=1, source_target_pairs={{0,12},{2,14},{4,8},{6,10},{8,4},{10,6},{12,0},{14,2},{1,13},{3,15... | collective-permute-start | bytes 233480 | tf_op jit(solution)/shard_map/ppermute | solution.py:186
  39.9 4.3 %collective-permute-start.2 = (f32[152,128]{1,0:T(8,128)S(1)}, f32[152,128]{1,0:T(8,128)S(1)}, u32[]{:S(2)}, u32[]{:S(2)}) collective-permute-start(f32[152,128]{1,0:T(8,128)S(1)} %add.16), channel_id=1, source_target_pairs={{0,4},{2,6},{4,0},{6,2},{8,12},{10,14},{12,8},{14,10},{1,5},{3,7},... | collective-permute-start | bytes 233480 | tf_op jit(solution)/shard_map/ppermute | solution.py:186
  44.2 0.0 all-to-all-done.1.parts_ref
  44.2 8.9 %right_root.1 = f32[8,152,128]{2,1,0:T(8,128)} custom-call(f32[4,152,128]{2,1,0:T(8,128)S(1)} %all-to-all-done.1.parts_ref), custom_call_target="tpu_custom_call" | custom-call | flops 16000000000 | bytes 1048576 | tf_op jit(solution)/shard_map/right_root/pallas_call | solution.py:214
  53.1 0.0 collective-permute-done.4
  53.1 0.0 collective-permute-done.3
  53.1 0.0 collective-permute-done.2
  53.1 5.7 %all-to-all-start.2 = ((f32[8,152,128]{2,1,0:T(8,128)}), f32[8,152,128]{2,1,0:T(8,128)S(1)}, u32[]{:S(2)}, u32[]{:S(2)}) async-start(f32[8,152,128]{2,1,0:T(8,128)} %right_root.1), calls=%async_computation.2 | async-start | bytes 1245184 | tf_op jit(solution)/shard_map/all_to_all | solution.py:190
  58.8 0.0 copy-done.1
  58.8 8.8 %left_root.1 = (bf16[8,192,192]{2,1,0:T(8,128)(2,1)S(1)}, bf16[8,192,192]{2,1,0:T(8,128)(2,1)S(1)}) custom-call(f32[152,128]{1,0:T(8,128)S(1)} %add_add_fusion.gram_ref, f32[192,1536]{1,0:T(8,128)S(1)} %copy-done.1), custom_call_target="tpu_custom_call" | custom-call | flops 8000000000 | bytes 1048576 | tf_op jit(solution)/shard_map/left_root/pallas_call | solution.py:226
  67.6 0.0 all-to-all-done.2.roots_ref
  67.7 2.6 %update.1 = f32[192,1536]{1,0:T(8,128)} custom-call(bf16[8,192,192]{2,1,0:T(8,128)(2,1)S(1)} %get-tuple-element.24.high_ref, bf16[8,192,192]{2,1,0:T(8,128)(2,1)S(1)} %get-tuple-element.25.low_ref, f32[8,152,128]{2,1,0:T(8,128)S(1)} %all-to-all-done.2.roots_ref), custom_call_target="tpu_custom_call" | custom-call | tf_op jit(solution)/shard_map/update/pallas_call | solution.py:234
  (5 shorter events, 0.1 us)
Async XLA Ops:
  0.0 1.3 %copy-start = (f32[192,1536]{1,0:T(8,128)S(1)}, f32[192,1536]{1,0:T(8,128)}, u32[]{:S(2)}) copy-start(f32[192,1536]{1,0:T(8,128)} %grad_ref.3) | copy-start | bytes 3538948
  3.6 15.9 %all-to-all-start = ((f32[8,152,128]{2,1,0:T(8,128)}), f32[8,152,128]{2,1,0:T(8,128)S(1)}, u32[]{:S(2)}, u32[]{:S(2)}) async-start(f32[8,152,128]{2,1,0:T(8,128)} %get-tuple-element.16), calls=%async_computation | async-start | bytes 1245184 | tf_op jit(solution)/shard_map/all_to_all | solution.py:190
  9.4 3.2 %collective-permute-start = (f32[152,128]{1,0:T(8,128)S(1)}, f32[152,128]{1,0:T(8,128)S(1)}, u32[]{:S(2)}, u32[]{:S(2)}) collective-permute-start(f32[152,128]{1,0:T(8,128)S(1)} %get-tuple-element.17), channel_id=1, source_target_pairs={{0,1},{1,0},{2,3},{3,2},{4,5},{5,4},{6,7},{7,6},{8,9},{9,8},{10,11... | collective-permute-start | bytes 233480 | tf_op jit(solution)/shard_map/ppermute | solution.py:186
  12.6 7.0 %collective-permute-start.1 = (f32[152,128]{1,0:T(8,128)S(1)}, f32[152,128]{1,0:T(8,128)S(1)}, u32[]{:S(2)}, u32[]{:S(2)}) collective-permute-start(f32[152,128]{1,0:T(8,128)S(1)} %add.15), channel_id=1, source_target_pairs={{0,2},{2,0},{4,6},{6,4},{8,10},{10,8},{12,14},{14,12},{1,3},{3,1},... | collective-permute-start | bytes 233480 | tf_op jit(solution)/shard_map/ppermute | solution.py:186
  20.3 23.9 %all-to-all-start.1 = ((f32[4,152,128]{2,1,0:T(8,128)}), f32[4,152,128]{2,1,0:T(8,128)S(1)}, u32[]{:S(2)}, u32[]{:S(2)}) async-start(f32[4,152,128]{2,1,0:T(8,128)} %broadcast_in_dim.2), calls=%async_computation.1 | async-start | bytes 622592 | tf_op jit(solution)/shard_map/all_to_all | solution.py:190
  27.6 25.5 %collective-permute-start.4 = (f32[152,128]{1,0:T(8,128)S(1)}, f32[152,128]{1,0:T(8,128)S(1)}, u32[]{:S(2)}, u32[]{:S(2)}) collective-permute-start(f32[152,128]{1,0:T(8,128)S(1)} %add.16), channel_id=1, source_target_pairs={{0,8},{2,10},{4,12},{6,14},{8,0},{10,2},{12,4},{14,6},{1,9},{3,11}... | collective-permute-start | bytes 233480 | tf_op jit(solution)/shard_map/ppermute | solution.py:186
  38.0 15.1 %collective-permute-start.3 = (f32[152,128]{1,0:T(8,128)S(1)}, f32[152,128]{1,0:T(8,128)S(1)}, u32[]{:S(2)}, u32[]{:S(2)}) collective-permute-start(f32[152,128]{1,0:T(8,128)S(1)} %add.16), channel_id=1, source_target_pairs={{0,12},{2,14},{4,8},{6,10},{8,4},{10,6},{12,0},{14,2},{1,13},{3,15... | collective-permute-start | bytes 233480 | tf_op jit(solution)/shard_map/ppermute | solution.py:186
  39.9 13.2 %collective-permute-start.2 = (f32[152,128]{1,0:T(8,128)S(1)}, f32[152,128]{1,0:T(8,128)S(1)}, u32[]{:S(2)}, u32[]{:S(2)}) collective-permute-start(f32[152,128]{1,0:T(8,128)S(1)} %add.16), channel_id=1, source_target_pairs={{0,4},{2,6},{4,0},{6,2},{8,12},{10,14},{12,8},{14,10},{1,5},{3,7},... | collective-permute-start | bytes 233480 | tf_op jit(solution)/shard_map/ppermute | solution.py:186
  53.1 5.7 %copy-start.1 = (f32[192,1536]{1,0:T(8,128)S(1)}, f32[192,1536]{1,0:T(8,128)}, u32[]{:S(2)}) copy-start(f32[192,1536]{1,0:T(8,128)} %grad_ref.3) | copy-start | bytes 3538948
  53.1 14.5 %all-to-all-start.2 = ((f32[8,152,128]{2,1,0:T(8,128)}), f32[8,152,128]{2,1,0:T(8,128)S(1)}, u32[]{:S(2)}, u32[]{:S(2)}) async-start(f32[8,152,128]{2,1,0:T(8,128)} %right_root.1), calls=%async_computation.2 | async-start | bytes 1245184 | tf_op jit(solution)/shard_map/all_to_all | solution.py:190

commit v9 on v8

--- a/solution.py
+++ b/solution.py
@@ -93,8 +93,10 @@
 
     def advance(m):
         parts = split(m)
+        centred = (m - 0.5 * identity).astype(BF16)
         excess = [
-            split(0.0625 * product((parts[0][b], parts[1][b]), parts) - 0.625 * m[b]) for b in bands
+            split(0.0625 * dot(centred[b], centred) - 0.015625 * identity[b] - 0.5625 * m[b])
+            for b in bands
         ]
         halfway = [1.5625 * m[b] + product(e, parts) for e, b in zip(excess, bands)]
         whole = [jnp.concatenate([e[k] for e in excess], axis=0) for k in range(2)]
@@ -111,8 +113,9 @@
 
     def step(k, carry):
         parts, following = advance(m_ref[...])
+        grown = grow(parts)
         m_ref[...] = following
-        x_ref[...] = grow(parts)
+        x_ref[...] = grown
         return carry
 
     lax.fori_loop(0, ITERS - 2, step, 0, unroll=True)

time: 70.9 us -> 69.5 us (0.980)
  Pallas kernels: 22.7 us -> 21.2 us
    pallas_call x1, Pallas kernels: 8.8 us -> 8.09 us  [body(): pl.pallas_call(left_root_kernel, out_shape=[shape(count, height, BLOCK, d...]
  transfers between devices with their start and end apart: 8 -> 8, of which waited for: 2 -> 2; matrix products, arithmetic and copies ran while one was open for 0% -> 0% of each run, Pallas kernels for 25% -> 24%
where the time goes in v9:
time: 69.5 us; the launch traced here: 69 us
  starting transfers between devices  41.5 us (60%)
  Pallas kernels  21.2 us (31%)
  waiting for transfers between devices  3.91 us (6%)
  local copies, waits for them, and re-layouts  2.01 us (3%)
    ppermute x5, starting transfers between devices, partner(): lax.ppermute(x, axis, [(i, i ^ bits) for i in range(lax.axis_size(axis))])  22.7 us
    all_to_all x3, starting transfers between devices, swap(): return lax.all_to_all(x, axes, 0, 0, tiled=True)  18.8 us
    pallas_call x1, Pallas kernels, body(): pl.pallas_call(right_root_kernel, out_shape=shape(count, PACKED, LANES),...  8.2 us
    pallas_call x1, Pallas kernels, body(): pl.pallas_call(left_root_kernel, out_shape=[shape(count, height, BLOCK, d...  8.09 us
    ppermute x5, waiting for transfers between devices, partner(): lax.ppermute(x, axis, [(i, i ^ bits) for i in range(lax.axis_size(axis))])  3.91 us
    pallas_call x1, Pallas kernels, body(): pl.pallas_call(update_kernel, out_specs=pl.BlockSpec(memory_space=pl.ANY)...  2.59 us
    pallas_call x1, Pallas kernels, body(): pl.pallas_call(gram_kernel, out_shape=[shape(PACKED, LANES), shape(count,...  2.36 us
  transfers between devices with their start and end apart: 8, of which 2 were waited for; matrix products, arithmetic and copies ran while one was open for 0% of the time, Pallas kernels for 24%

profile of v9, /device:TPU:40, one launch (start us, length us, event | category | flops | bytes accessed | tf_op | source)
XLA Modules:
  0.0 69.0 jit_solution(17840636100894100191)
XLA Ops:
  0.0 0.0 copy-start
  0.0 1.3 %copy-done = f32[192,1536]{1,0:T(8,128)S(1)} copy-done((f32[192,1536]{1,0:T(8,128)S(1)}, f32[192,1536]{1,0:T(8,128)}, u32[]{:S(2)}) %copy-start) | copy-done | bytes 1179672
  1.3 2.4 %grams.1 = (f32[152,128]{1,0:T(8,128)S(1)}, f32[8,152,128]{2,1,0:T(8,128)}) custom-call(f32[192,1536]{1,0:T(8,128)S(1)} %copy-done), custom_call_target="tpu_custom_call" | custom-call | tf_op jit(solution)/shard_map/grams/pallas_call | solution.py:204
  3.6 5.8 %all-to-all-start = ((f32[8,152,128]{2,1,0:T(8,128)}), f32[8,152,128]{2,1,0:T(8,128)S(1)}, u32[]{:S(2)}, u32[]{:S(2)}) async-start(f32[8,152,128]{2,1,0:T(8,128)} %get-tuple-element.16), calls=%async_computation | async-start | bytes 1245184 | tf_op jit(solution)/shard_map/all_to_all | solution.py:193
  9.4 1.9 %collective-permute-start = (f32[152,128]{1,0:T(8,128)S(1)}, f32[152,128]{1,0:T(8,128)S(1)}, u32[]{:S(2)}, u32[]{:S(2)}) collective-permute-start(f32[152,128]{1,0:T(8,128)S(1)} %get-tuple-element.17), channel_id=1, source_target_pairs={{0,1},{1,0},{2,3},{3,2},{4,5},{5,4},{6,7},{7,6},{8,9},{9,8},{10,11... | collective-permute-start | bytes 233480 | tf_op jit(solution)/shard_map/ppermute | solution.py:189
  11.3 1.2 %collective-permute-done = f32[152,128]{1,0:T(8,128)S(1)} collective-permute-done((f32[152,128]{1,0:T(8,128)S(1)}, f32[152,128]{1,0:T(8,128)S(1)}, u32[]{:S(2)}, u32[]{:S(2)}) %collective-permute-start) | collective-permute-done | bytes 77856 | tf_op jit(solution)/shard_map/ppermute | solution.py:189
  12.6 4.3 %collective-permute-start.1 = (f32[152,128]{1,0:T(8,128)S(1)}, f32[152,128]{1,0:T(8,128)S(1)}, u32[]{:S(2)}, u32[]{:S(2)}) collective-permute-start(f32[152,128]{1,0:T(8,128)S(1)} %add.15), channel_id=1, source_target_pairs={{0,2},{2,0},{4,6},{6,4},{8,10},{10,8},{12,14},{14,12},{1,3},{3,1},... | collective-permute-start | bytes 233480 | tf_op jit(solution)/shard_map/ppermute | solution.py:189
  16.9 2.7 %collective-permute-done.1 = f32[152,128]{1,0:T(8,128)S(1)} collective-permute-done((f32[152,128]{1,0:T(8,128)S(1)}, f32[152,128]{1,0:T(8,128)S(1)}, u32[]{:S(2)}, u32[]{:S(2)}) %collective-permute-start.1) | collective-permute-done | bytes 77856 | tf_op jit(solution)/shard_map/ppermute | solution.py:189
  19.5 0.0 all-to-all-done
  19.6 0.7 %broadcast_in_dim.2 = f32[4,152,128]{2,1,0:T(8,128)} broadcast(f32[152,128]{1,0:T(8,128)S(1)} %reduce_sum.9), dimensions={1,2} | broadcast | bytes 389120 | tf_op jit(solution)/shard_map/broadcast_in_dim | solution.py:214
  20.3 7.3 %all-to-all-start.1 = ((f32[4,152,128]{2,1,0:T(8,128)}), f32[4,152,128]{2,1,0:T(8,128)S(1)}, u32[]{:S(2)}, u32[]{:S(2)}) async-start(f32[4,152,128]{2,1,0:T(8,128)} %broadcast_in_dim.2), calls=%async_computation.1 | async-start | bytes 622592 | tf_op jit(solution)/shard_map/all_to_all | solution.py:193
  27.6 10.3 %collective-permute-start.4 = (f32[152,128]{1,0:T(8,128)S(1)}, f32[152,128]{1,0:T(8,128)S(1)}, u32[]{:S(2)}, u32[]{:S(2)}) collective-permute-start(f32[152,128]{1,0:T(8,128)S(1)} %add.16), channel_id=1, source_target_pairs={{0,8},{2,10},{4,12},{6,14},{8,0},{10,2},{12,4},{14,6},{1,9},{3,11}... | collective-permute-start | bytes 233480 | tf_op jit(solution)/shard_map/ppermute | solution.py:189
  38.0 1.9 %collective-permute-start.3 = (f32[152,128]{1,0:T(8,128)S(1)}, f32[152,128]{1,0:T(8,128)S(1)}, u32[]{:S(2)}, u32[]{:S(2)}) collective-permute-start(f32[152,128]{1,0:T(8,128)S(1)} %add.16), channel_id=1, source_target_pairs={{0,12},{2,14},{4,8},{6,10},{8,4},{10,6},{12,0},{14,2},{1,13},{3,15... | collective-permute-start | bytes 233480 | tf_op jit(solution)/shard_map/ppermute | solution.py:189
  39.9 4.3 %collective-permute-start.2 = (f32[152,128]{1,0:T(8,128)S(1)}, f32[152,128]{1,0:T(8,128)S(1)}, u32[]{:S(2)}, u32[]{:S(2)}) collective-permute-start(f32[152,128]{1,0:T(8,128)S(1)} %add.16), channel_id=1, source_target_pairs={{0,4},{2,6},{4,0},{6,2},{8,12},{10,14},{12,8},{14,10},{1,5},{3,7},... | collective-permute-start | bytes 233480 | tf_op jit(solution)/shard_map/ppermute | solution.py:189
  44.2 0.0 all-to-all-done.1.parts_ref
  44.2 8.2 %right_root.1 = f32[8,152,128]{2,1,0:T(8,128)} custom-call(f32[4,152,128]{2,1,0:T(8,128)S(1)} %all-to-all-done.1.parts_ref), custom_call_target="tpu_custom_call" | custom-call | flops 16000000000 | bytes 1048576 | tf_op jit(solution)/shard_map/right_root/pallas_call | solution.py:217
  52.4 0.0 collective-permute-done.4
  52.4 0.0 collective-permute-done.3
  52.4 0.0 collective-permute-done.2
  52.4 5.7 %all-to-all-start.2 = ((f32[8,152,128]{2,1,0:T(8,128)}), f32[8,152,128]{2,1,0:T(8,128)S(1)}, u32[]{:S(2)}, u32[]{:S(2)}) async-start(f32[8,152,128]{2,1,0:T(8,128)} %right_root.1), calls=%async_computation.2 | async-start | bytes 1245184 | tf_op jit(solution)/shard_map/all_to_all | solution.py:193
  58.1 0.0 copy-done.1
  58.1 8.1 %left_root.1 = (bf16[8,192,192]{2,1,0:T(8,128)(2,1)S(1)}, bf16[8,192,192]{2,1,0:T(8,128)(2,1)S(1)}) custom-call(f32[152,128]{1,0:T(8,128)S(1)} %add_add_fusion.gram_ref, f32[192,1536]{1,0:T(8,128)S(1)} %copy-done.1), custom_call_target="tpu_custom_call" | custom-call | flops 8000000000 | bytes 1048576 | tf_op jit(solution)/shard_map/left_root/pallas_call | solution.py:229
  66.2 0.0 all-to-all-done.2.roots_ref
  66.3 2.6 %update.1 = f32[192,1536]{1,0:T(8,128)} custom-call(bf16[8,192,192]{2,1,0:T(8,128)(2,1)S(1)} %get-tuple-element.24.high_ref, bf16[8,192,192]{2,1,0:T(8,128)(2,1)S(1)} %get-tuple-element.25.low_ref, f32[8,152,128]{2,1,0:T(8,128)S(1)} %all-to-all-done.2.roots_ref), custom_call_target="tpu_custom_call" | custom-call | tf_op jit(solution)/shard_map/update/pallas_call | solution.py:237
  (5 shorter events, 0.1 us)
Async XLA Ops:
  0.0 1.3 %copy-start = (f32[192,1536]{1,0:T(8,128)S(1)}, f32[192,1536]{1,0:T(8,128)}, u32[]{:S(2)}) copy-start(f32[192,1536]{1,0:T(8,128)} %grad_ref.3) | copy-start | bytes 3538948
  3.6 15.9 %all-to-all-start = ((f32[8,152,128]{2,1,0:T(8,128)}), f32[8,152,128]{2,1,0:T(8,128)S(1)}, u32[]{:S(2)}, u32[]{:S(2)}) async-start(f32[8,152,128]{2,1,0:T(8,128)} %get-tuple-element.16), calls=%async_computation | async-start | bytes 1245184 | tf_op jit(solution)/shard_map/all_to_all | solution.py:193
  9.4 3.2 %collective-permute-start = (f32[152,128]{1,0:T(8,128)S(1)}, f32[152,128]{1,0:T(8,128)S(1)}, u32[]{:S(2)}, u32[]{:S(2)}) collective-permute-start(f32[152,128]{1,0:T(8,128)S(1)} %get-tuple-element.17), channel_id=1, source_target_pairs={{0,1},{1,0},{2,3},{3,2},{4,5},{5,4},{6,7},{7,6},{8,9},{9,8},{10,11... | collective-permute-start | bytes 233480 | tf_op jit(solution)/shard_map/ppermute | solution.py:189
  12.6 7.0 %collective-permute-start.1 = (f32[152,128]{1,0:T(8,128)S(1)}, f32[152,128]{1,0:T(8,128)S(1)}, u32[]{:S(2)}, u32[]{:S(2)}) collective-permute-start(f32[152,128]{1,0:T(8,128)S(1)} %add.15), channel_id=1, source_target_pairs={{0,2},{2,0},{4,6},{6,4},{8,10},{10,8},{12,14},{14,12},{1,3},{3,1},... | collective-permute-start | bytes 233480 | tf_op jit(solution)/shard_map/ppermute | solution.py:189
  20.3 23.9 %all-to-all-start.1 = ((f32[4,152,128]{2,1,0:T(8,128)}), f32[4,152,128]{2,1,0:T(8,128)S(1)}, u32[]{:S(2)}, u32[]{:S(2)}) async-start(f32[4,152,128]{2,1,0:T(8,128)} %broadcast_in_dim.2), calls=%async_computation.1 | async-start | bytes 622592 | tf_op jit(solution)/shard_map/all_to_all | solution.py:193
  27.6 24.8 %collective-permute-start.4 = (f32[152,128]{1,0:T(8,128)S(1)}, f32[152,128]{1,0:T(8,128)S(1)}, u32[]{:S(2)}, u32[]{:S(2)}) collective-permute-start(f32[152,128]{1,0:T(8,128)S(1)} %add.16), channel_id=1, source_target_pairs={{0,8},{2,10},{4,12},{6,14},{8,0},{10,2},{12,4},{14,6},{1,9},{3,11}... | collective-permute-start | bytes 233480 | tf_op jit(solution)/shard_map/ppermute | solution.py:189
  38.0 14.5 %collective-permute-start.3 = (f32[152,128]{1,0:T(8,128)S(1)}, f32[152,128]{1,0:T(8,128)S(1)}, u32[]{:S(2)}, u32[]{:S(2)}) collective-permute-start(f32[152,128]{1,0:T(8,128)S(1)} %add.16), channel_id=1, source_target_pairs={{0,12},{2,14},{4,8},{6,10},{8,4},{10,6},{12,0},{14,2},{1,13},{3,15... | collective-permute-start | bytes 233480 | tf_op jit(solution)/shard_map/ppermute | solution.py:189
  39.9 12.5 %collective-permute-start.2 = (f32[152,128]{1,0:T(8,128)S(1)}, f32[152,128]{1,0:T(8,128)S(1)}, u32[]{:S(2)}, u32[]{:S(2)}) collective-permute-start(f32[152,128]{1,0:T(8,128)S(1)} %add.16), channel_id=1, source_target_pairs={{0,4},{2,6},{4,0},{6,2},{8,12},{10,14},{12,8},{14,10},{1,5},{3,7},... | collective-permute-start | bytes 233480 | tf_op jit(solution)/shard_map/ppermute | solution.py:189
  52.4 5.7 %copy-start.1 = (f32[192,1536]{1,0:T(8,128)S(1)}, f32[192,1536]{1,0:T(8,128)}, u32[]{:S(2)}) copy-start(f32[192,1536]{1,0:T(8,128)} %grad_ref.3) | copy-start | bytes 3538948
  52.4 13.8 %all-to-all-start.2 = ((f32[8,152,128]{2,1,0:T(8,128)}), f32[8,152,128]{2,1,0:T(8,128)S(1)}, u32[]{:S(2)}, u32[]{:S(2)}) async-start(f32[8,152,128]{2,1,0:T(8,128)} %right_root.1), calls=%async_computation.2 | async-start | bytes 1245184 | tf_op jit(solution)/shard_map/all_to_all | solution.py:193

commit v10 on v9

--- a/solution.py
+++ b/solution.py
@@ -70,17 +70,15 @@
     )
 
 
-def gram_kernel(grad_ref, left_ref, right_ref):
-    rows, columns = ((0,), (0,)), ((1,), (1,))
-    left = None
-    for k in range(grad_ref.shape[1] // CHUNK):
-        g = split(grad_ref[:, k * CHUNK : (k + 1) * CHUNK])
-        part = product(g, g, columns)
-        left = part if k == 0 else left + part
-        for c in range(CHUNK // BLOCK):
-            h = [part[:, c * BLOCK : (c + 1) * BLOCK] for part in g]
-            right_ref[k * (CHUNK // BLOCK) + c] = pack(product(h, h, rows))
-    left_ref[...] = pack(left)
+def right_gram_kernel(grad_ref, right_ref):
+    for c in range(right_ref.shape[0]):
+        h = split(grad_ref[:, c * BLOCK : (c + 1) * BLOCK])
+        right_ref[c] = pack(product(h, h, ((0,), (0,))))
+
+
+def left_gram_kernel(grad_ref, left_ref):
+    g = split(grad_ref[...])
+    left_ref[...] = pack(product(g, g, ((1,), (1,))))
 
 
 def newton(gram, m_ref, x_ref):
@@ -201,11 +199,18 @@
     square = [pltpu.VMEM((BLOCK, BLOCK), F32)] * 2
     whole = [pltpu.VMEM((chunks, height, CHUNK), F32), pltpu.SemaphoreType.DMA((chunks,))]
 
-    left, right = pl.pallas_call(
-        gram_kernel,
-        out_shape=[shape(PACKED, LANES), shape(count, PACKED, LANES)],
-        compiler_params=PARAMS,
-        name="grams",
+    right = pl.pallas_call(
+        right_gram_kernel,
+        out_shape=shape(count, PACKED, LANES),
+        compiler_params=PARAMS,
+        name="right_gram",
+    )(gradient)
+    left = pl.pallas_call(
+        left_gram_kernel,
+        out_shape=shape(PACKED, LANES),
+        compiler_params=PARAMS,
+        name="left_gram",
+        cost_estimate=estimate(10**9),
     )(gradient)
     right = swap(right, group)
     left = left + partner(left, "core", 1)

time: 69.5 us -> 70.3 us (1.012)
  Pallas kernels: 21.2 us -> 22.2 us
    pallas_call x1 -> x2, Pallas kernels: 2.36 us -> 3.29 us  [the longest x1 2.57 us: body(): pl.pallas_call(right_gram_kernel, out_shape=shape(count, PACKED, LANES),...]
where the time goes in v10:
time: 70.3 us; the launch traced here: 69.8 us
  starting transfers between devices  41.4 us (59%)
  Pallas kernels  22.2 us (32%)
  waiting for transfers between devices  3.91 us (6%)
  local copies, waits for them, and re-layouts  2.01 us (3%)
    ppermute x5, starting transfers between devices, partner(): lax.ppermute(x, axis, [(i, i ^ bits) for i in range(lax.axis_size(axis))])  22.6 us
    all_to_all x3, starting transfers between devices, swap(): return lax.all_to_all(x, axes, 0, 0, tiled=True)  18.8 us
    pallas_call x1, Pallas kernels, body(): pl.pallas_call(right_root_kernel, out_shape=shape(count, PACKED, LANES),...  8.21 us
    pallas_call x1, Pallas kernels, body(): pl.pallas_call(left_root_kernel, out_shape=[shape(count, height, BLOCK, d...  8.09 us
    ppermute x5, waiting for transfers between devices, partner(): lax.ppermute(x, axis, [(i, i ^ bits) for i in range(lax.axis_size(axis))])  3.91 us
    pallas_call x1, Pallas kernels, body(): pl.pallas_call(update_kernel, out_specs=pl.BlockSpec(memory_space=pl.ANY)...  2.59 us
    pallas_call x1, Pallas kernels, body(): pl.pallas_call(right_gram_kernel, out_shape=shape(count, PACKED, LANES),...  2.57 us
  transfers between devices with their start and end apart: 8, of which 2 were waited for; matrix products, arithmetic and copies ran while one was open for 0% of the time, Pallas kernels for 24%

profile of v10, /device:TPU:40, one launch (start us, length us, event | category | flops | bytes accessed | tf_op | source)
XLA Modules:
  0.0 69.8 jit_solution(8588154120735146889)
XLA Ops:
  0.0 1.3 %copy-done = f32[192,1536]{1,0:T(8,128)S(1)} copy-done((f32[192,1536]{1,0:T(8,128)S(1)}, f32[192,1536]{1,0:T(8,128)}, u32[]{:S(2)}) %copy-start) | copy-done | bytes 1179672
  1.3 2.6 %right_gram.1 = f32[8,152,128]{2,1,0:T(8,128)} custom-call(f32[192,1536]{1,0:T(8,128)S(1)} %copy-done), custom_call_target="tpu_custom_call" | custom-call | tf_op jit(solution)/shard_map/right_gram/pallas_call | solution.py:202
  3.8 5.8 %all-to-all-start = ((f32[8,152,128]{2,1,0:T(8,128)}), f32[8,152,128]{2,1,0:T(8,128)S(1)}, u32[]{:S(2)}, u32[]{:S(2)}) async-start(f32[8,152,128]{2,1,0:T(8,128)} %right_gram.1), calls=%async_computation | async-start | bytes 1245184 | tf_op jit(solution)/shard_map/all_to_all | solution.py:191
  9.6 0.0 copy-done.1
  9.6 0.7 %left_gram.1 = f32[152,128]{1,0:T(8,128)S(1)} custom-call(f32[192,1536]{1,0:T(8,128)S(1)} %copy-done.1), custom_call_target="tpu_custom_call" | custom-call | flops 1000000000 | bytes 1048576 | tf_op jit(solution)/shard_map/left_gram/pallas_call | solution.py:208
  10.3 1.9 %collective-permute-start = (f32[152,128]{1,0:T(8,128)S(1)}, f32[152,128]{1,0:T(8,128)S(1)}, u32[]{:S(2)}, u32[]{:S(2)}) collective-permute-start(f32[152,128]{1,0:T(8,128)S(1)} %left_gram.1), channel_id=1, source_target_pairs={{0,1},{1,0},{2,3},{3,2},{4,5},{5,4},{6,7},{7,6},{8,9},{9,8},{10,11... | collective-permute-start | bytes 233480 | tf_op jit(solution)/shard_map/ppermute | solution.py:187
  12.3 1.2 %collective-permute-done = f32[152,128]{1,0:T(8,128)S(1)} collective-permute-done((f32[152,128]{1,0:T(8,128)S(1)}, f32[152,128]{1,0:T(8,128)S(1)}, u32[]{:S(2)}, u32[]{:S(2)}) %collective-permute-start) | collective-permute-done | bytes 77856 | tf_op jit(solution)/shard_map/ppermute | solution.py:187
  13.5 4.3 %collective-permute-start.1 = (f32[152,128]{1,0:T(8,128)S(1)}, f32[152,128]{1,0:T(8,128)S(1)}, u32[]{:S(2)}, u32[]{:S(2)}) collective-permute-start(f32[152,128]{1,0:T(8,128)S(1)} %add.15), channel_id=1, source_target_pairs={{0,2},{2,0},{4,6},{6,4},{8,10},{10,8},{12,14},{14,12},{1,3},{3,1},... | collective-permute-start | bytes 233480 | tf_op jit(solution)/shard_map/ppermute | solution.py:187
  17.8 2.7 %collective-permute-done.1 = f32[152,128]{1,0:T(8,128)S(1)} collective-permute-done((f32[152,128]{1,0:T(8,128)S(1)}, f32[152,128]{1,0:T(8,128)S(1)}, u32[]{:S(2)}, u32[]{:S(2)}) %collective-permute-start.1) | collective-permute-done | bytes 77856 | tf_op jit(solution)/shard_map/ppermute | solution.py:187
  20.5 0.0 all-to-all-done
  20.5 0.7 %broadcast_in_dim.2 = f32[4,152,128]{2,1,0:T(8,128)} broadcast(f32[152,128]{1,0:T(8,128)S(1)} %reduce_sum.9), dimensions={1,2} | broadcast | bytes 389120 | tf_op jit(solution)/shard_map/broadcast_in_dim | solution.py:219
  21.3 7.3 %all-to-all-start.1 = ((f32[4,152,128]{2,1,0:T(8,128)}), f32[4,152,128]{2,1,0:T(8,128)S(1)}, u32[]{:S(2)}, u32[]{:S(2)}) async-start(f32[4,152,128]{2,1,0:T(8,128)} %broadcast_in_dim.2), calls=%async_computation.1 | async-start | bytes 622592 | tf_op jit(solution)/shard_map/all_to_all | solution.py:191
  28.6 10.1 %collective-permute-start.4 = (f32[152,128]{1,0:T(8,128)S(1)}, f32[152,128]{1,0:T(8,128)S(1)}, u32[]{:S(2)}, u32[]{:S(2)}) collective-permute-start(f32[152,128]{1,0:T(8,128)S(1)} %add.16), channel_id=1, source_target_pairs={{0,8},{2,10},{4,12},{6,14},{8,0},{10,2},{12,4},{14,6},{1,9},{3,11}... | collective-permute-start | bytes 233480 | tf_op jit(solution)/shard_map/ppermute | solution.py:187
  38.7 1.9 %collective-permute-start.3 = (f32[152,128]{1,0:T(8,128)S(1)}, f32[152,128]{1,0:T(8,128)S(1)}, u32[]{:S(2)}, u32[]{:S(2)}) collective-permute-start(f32[152,128]{1,0:T(8,128)S(1)} %add.16), channel_id=1, source_target_pairs={{0,12},{2,14},{4,8},{6,10},{8,4},{10,6},{12,0},{14,2},{1,13},{3,15... | collective-permute-start | bytes 233480 | tf_op jit(solution)/shard_map/ppermute | solution.py:187
  40.7 4.3 %collective-permute-start.2 = (f32[152,128]{1,0:T(8,128)S(1)}, f32[152,128]{1,0:T(8,128)S(1)}, u32[]{:S(2)}, u32[]{:S(2)}) collective-permute-start(f32[152,128]{1,0:T(8,128)S(1)} %add.16), channel_id=1, source_target_pairs={{0,4},{2,6},{4,0},{6,2},{8,12},{10,14},{12,8},{14,10},{1,5},{3,7},... | collective-permute-start | bytes 233480 | tf_op jit(solution)/shard_map/ppermute | solution.py:187
  45.0 0.0 all-to-all-done.1.parts_ref
  45.0 8.2 %right_root.1 = f32[8,152,128]{2,1,0:T(8,128)} custom-call(f32[4,152,128]{2,1,0:T(8,128)S(1)} %all-to-all-done.1.parts_ref), custom_call_target="tpu_custom_call" | custom-call | flops 16000000000 | bytes 1048576 | tf_op jit(solution)/shard_map/right_root/pallas_call | solution.py:222
  53.2 0.0 collective-permute-done.4
  53.2 0.0 collective-permute-done.3
  53.2 0.0 collective-permute-done.2
  53.2 5.7 %all-to-all-start.2 = ((f32[8,152,128]{2,1,0:T(8,128)}), f32[8,152,128]{2,1,0:T(8,128)S(1)}, u32[]{:S(2)}, u32[]{:S(2)}) async-start(f32[8,152,128]{2,1,0:T(8,128)} %right_root.1), calls=%async_computation.2 | async-start | bytes 1245184 | tf_op jit(solution)/shard_map/all_to_all | solution.py:191
  59.0 8.1 %left_root.1 = (bf16[8,192,192]{2,1,0:T(8,128)(2,1)S(1)}, bf16[8,192,192]{2,1,0:T(8,128)(2,1)S(1)}) custom-call(f32[152,128]{1,0:T(8,128)S(1)} %add_add_fusion.gram_ref, f32[192,1536]{1,0:T(8,128)S(1)} %copy-done.1), custom_call_target="tpu_custom_call" | custom-call | flops 8000000000 | bytes 1048576 | tf_op jit(solution)/shard_map/left_root/pallas_call | solution.py:234
  67.0 0.0 all-to-all-done.2.roots_ref
  67.1 2.6 %update.1 = f32[192,1536]{1,0:T(8,128)} custom-call(bf16[8,192,192]{2,1,0:T(8,128)(2,1)S(1)} %get-tuple-element.20.high_ref, bf16[8,192,192]{2,1,0:T(8,128)(2,1)S(1)} %get-tuple-element.21.low_ref, f32[8,152,128]{2,1,0:T(8,128)S(1)} %all-to-all-done.2.roots_ref), custom_call_target="tpu_custom_call" | custom-call | tf_op jit(solution)/shard_map/update/pallas_call | solution.py:242
  (6 shorter events, 0.1 us)
Async XLA Ops:
  0.0 1.3 %copy-start = (f32[192,1536]{1,0:T(8,128)S(1)}, f32[192,1536]{1,0:T(8,128)}, u32[]{:S(2)}) copy-start(f32[192,1536]{1,0:T(8,128)} %grad_ref.5) | copy-start | bytes 3538948
  1.3 8.3 %copy-start.1 = (f32[192,1536]{1,0:T(8,128)S(1)}, f32[192,1536]{1,0:T(8,128)}, u32[]{:S(2)}) copy-start(f32[192,1536]{1,0:T(8,128)} %grad_ref.5) | copy-start | bytes 3538948
  3.8 16.6 %all-to-all-start = ((f32[8,152,128]{2,1,0:T(8,128)}), f32[8,152,128]{2,1,0:T(8,128)S(1)}, u32[]{:S(2)}, u32[]{:S(2)}) async-start(f32[8,152,128]{2,1,0:T(8,128)} %right_gram.1), calls=%async_computation | async-start | bytes 1245184 | tf_op jit(solution)/shard_map/all_to_all | solution.py:191
  10.3 3.2 %collective-permute-start = (f32[152,128]{1,0:T(8,128)S(1)}, f32[152,128]{1,0:T(8,128)S(1)}, u32[]{:S(2)}, u32[]{:S(2)}) collective-permute-start(f32[152,128]{1,0:T(8,128)S(1)} %left_gram.1), channel_id=1, source_target_pairs={{0,1},{1,0},{2,3},{3,2},{4,5},{5,4},{6,7},{7,6},{8,9},{9,8},{10,11... | collective-permute-start | bytes 233480 | tf_op jit(solution)/shard_map/ppermute | solution.py:187
  13.5 7.0 %collective-permute-start.1 = (f32[152,128]{1,0:T(8,128)S(1)}, f32[152,128]{1,0:T(8,128)S(1)}, u32[]{:S(2)}, u32[]{:S(2)}) collective-permute-start(f32[152,128]{1,0:T(8,128)S(1)} %add.15), channel_id=1, source_target_pairs={{0,2},{2,0},{4,6},{6,4},{8,10},{10,8},{12,14},{14,12},{1,3},{3,1},... | collective-permute-start | bytes 233480 | tf_op jit(solution)/shard_map/ppermute | solution.py:187
  21.3 23.7 %all-to-all-start.1 = ((f32[4,152,128]{2,1,0:T(8,128)}), f32[4,152,128]{2,1,0:T(8,128)S(1)}, u32[]{:S(2)}, u32[]{:S(2)}) async-start(f32[4,152,128]{2,1,0:T(8,128)} %broadcast_in_dim.2), calls=%async_computation.1 | async-start | bytes 622592 | tf_op jit(solution)/shard_map/all_to_all | solution.py:191
  28.6 24.6 %collective-permute-start.4 = (f32[152,128]{1,0:T(8,128)S(1)}, f32[152,128]{1,0:T(8,128)S(1)}, u32[]{:S(2)}, u32[]{:S(2)}) collective-permute-start(f32[152,128]{1,0:T(8,128)S(1)} %add.16), channel_id=1, source_target_pairs={{0,8},{2,10},{4,12},{6,14},{8,0},{10,2},{12,4},{14,6},{1,9},{3,11}... | collective-permute-start | bytes 233480 | tf_op jit(solution)/shard_map/ppermute | solution.py:187
  38.7 14.4 %collective-permute-start.3 = (f32[152,128]{1,0:T(8,128)S(1)}, f32[152,128]{1,0:T(8,128)S(1)}, u32[]{:S(2)}, u32[]{:S(2)}) collective-permute-start(f32[152,128]{1,0:T(8,128)S(1)} %add.16), channel_id=1, source_target_pairs={{0,12},{2,14},{4,8},{6,10},{8,4},{10,6},{12,0},{14,2},{1,13},{3,15... | collective-permute-start | bytes 233480 | tf_op jit(solution)/shard_map/ppermute | solution.py:187
  40.7 12.5 %collective-permute-start.2 = (f32[152,128]{1,0:T(8,128)S(1)}, f32[152,128]{1,0:T(8,128)S(1)}, u32[]{:S(2)}, u32[]{:S(2)}) collective-permute-start(f32[152,128]{1,0:T(8,128)S(1)} %add.16), channel_id=1, source_target_pairs={{0,4},{2,6},{4,0},{6,2},{8,12},{10,14},{12,8},{14,10},{1,5},{3,7},... | collective-permute-start | bytes 233480 | tf_op jit(solution)/shard_map/ppermute | solution.py:187
  53.2 13.8 %all-to-all-start.2 = ((f32[8,152,128]{2,1,0:T(8,128)}), f32[8,152,128]{2,1,0:T(8,128)S(1)}, u32[]{:S(2)}, u32[]{:S(2)}) async-start(f32[8,152,128]{2,1,0:T(8,128)} %right_root.1), calls=%async_computation.2 | async-start | bytes 1245184 | tf_op jit(solution)/shard_map/all_to_all | solution.py:191
